TPU v7x, 32 devices: a whole 2x2x4 slice. The times are simulated.
32 devices in a mesh: groups: 2 (over x), chan: 16 (over z, y, core).
Axes of the slice: x: 2, y: 2, z: 4, core: 2. Of those that a mesh axis runs over, the one named last changes fastest.
Arguments:
- raw_strain: bfloat16 [8, 512, 4096], P(None, ('groups', 'chan')), parts along dimension 1, may hold values from -60 to 60
- bandpass: bfloat16 [64], replicated, may hold values from -0.75 to 0.75
- whiten_taps: bfloat16 [512, 64], P(('groups', 'chan')), parts along dimension 0, may hold values from -0.75 to 0.75
- segment_mask: int32 [8, 512], P(None, 'groups'), parts along dimension 1, may hold values from 0 to 1, as said below
- channel_block: int32 [512], P('groups'), parts along dimension 0, may hold values from 0 to 1, as said below
- source_block: int32 [2], P('groups'), parts along dimension 0, may hold values from 0 to 1
Outputs:
- correlations: bfloat16 [128, 512, 1024], P(None, ('groups', 'chan')), parts along dimension 1
There are 2 independent parts, one for each index of `groups`. A program takes and returns all parts, laid end to end along the dimension named above; an argument that names none is the same for every part. Nothing has to cross between parts.
Inputs may be any that keep to these rules, and one draw needn't show every extreme that they name: `segment_mask`: 1 marks a usable segment of a channel; some channels have no usable segment. `channel_block`: each block number is held by exactly 128 channels.
All inputs are finite; a program needn't handle non-finite values.
Results may differ from a plain program's by a relative error of at most 0.0093.
Values may be sent and summed in bfloat16 or wider, within the bound.
A program may use at most 64 MiB of HBM per device.

v0:
```python
import math

import jax
import jax.numpy as jnp
from jax import lax
from jax.sharding import PartitionSpec as P

SAMPLES = 4096
KLO = 64
FBINS = 512
LAGS = 1024
BLOCK = 128


def fir_matrix(coeffs):
    inner_idx = jnp.arange(256, dtype=jnp.int32)[:, None]
    outer_idx = jnp.arange(128, dtype=jnp.int32)[None, :]
    offset = outer_idx + 128 - inner_idx
    inside = (offset >= 0) & (offset < coeffs.shape[-1])
    picked = jnp.take(coeffs, jnp.clip(offset, 0, coeffs.shape[-1] - 1), axis=-1)
    return jnp.where(inside, picked, jnp.zeros_like(picked))


def fir_pass(signal, matrix, einsum_form):
    blocks = signal.reshape(signal.shape[:-1] + (signal.shape[-1] // 128, 128))
    joined = jnp.concatenate([jnp.roll(blocks, 1, axis=-2), blocks], axis=-1)
    result = jnp.einsum(einsum_form, joined, matrix, preferred_element_type=jnp.float32)
    return result.reshape(signal.shape)


def cross_stack(sources, receivers):
    turned = jnp.stack([-sources[:, :, 1], sources[:, :, 0]], axis=2)
    paired = jnp.stack([sources, turned], axis=0)
    return jnp.einsum("jgskf,grkf->srjf", paired, receivers, preferred_element_type=jnp.float32)


def body(raw_strain, bandpass, whiten_taps, segment_mask, channel_block, source_block):
    seg_count, chan_rows, sample_count = raw_strain.shape
    chan_start = lax.axis_index("chan") * chan_rows
    mask_all = segment_mask.astype(jnp.float32)
    mask_here = lax.dynamic_slice_in_dim(mask_all, chan_start, chan_rows, 1)
    filtered = fir_pass(raw_strain, fir_matrix(bandpass), "gcbi,io->gcbo")
    energy = jnp.mean(filtered * filtered, axis=-1, keepdims=True)
    normalized = (filtered / jnp.sqrt(energy + 1e-05)).astype(jnp.bfloat16)
    whitened = fir_pass(normalized, fir_matrix(whiten_taps), "gcbi,cio->gcbo").astype(jnp.bfloat16)
    time_rows = whitened.reshape(seg_count * chan_rows, sample_count)
    block_width = min(512, sample_count)
    bin_index = KLO + jnp.arange(FBINS, dtype=jnp.int32)

    def add_block(step_index, running):
        first_time = step_index * block_width
        piece_rows = lax.dynamic_slice_in_dim(time_rows, first_time, block_width, 1)
        sample_idx = first_time + jnp.arange(block_width, dtype=jnp.int32)
        phase_idx = sample_idx[:, None] * bin_index[None, :] % SAMPLES
        angles = phase_idx.astype(jnp.float32) * (2.0 * math.pi / SAMPLES)
        dft_table = jnp.concatenate(
            [jnp.cos(angles).astype(jnp.bfloat16), (-jnp.sin(angles)).astype(jnp.bfloat16)], axis=1
        )
        return running + jnp.dot(piece_rows, dft_table, preferred_element_type=jnp.float32)

    spectra = lax.fori_loop(
        0,
        sample_count // block_width,
        add_block,
        jnp.zeros((seg_count * chan_rows, 2 * FBINS), jnp.float32),
    )
    spectra = (
        spectra.reshape(seg_count, chan_rows, 2, FBINS) * mask_here[:, :, None, None]
    ).astype(jnp.bfloat16)
    member = channel_block == source_block[0]
    member_rank = jnp.cumsum(member.astype(jnp.int32)) - 1
    chosen = member[None, :] & (member_rank[None, :] == jnp.arange(BLOCK, dtype=jnp.int32)[:, None])
    selector = chosen.astype(jnp.bfloat16)
    source_mask = jnp.dot(mask_all, chosen.astype(jnp.float32).T)
    counts = jnp.dot(source_mask.T, mask_here)
    sources = jnp.einsum(
        "sc,gckf->gskf",
        selector,
        lax.all_gather(spectra, "chan", axis=1, tiled=True),
        preferred_element_type=jnp.float32,
    ).astype(jnp.bfloat16)
    stacked = cross_stack(sources, spectra).astype(jnp.bfloat16)
    lag_index = jnp.arange(LAGS, dtype=jnp.int32) - LAGS // 2
    lag_phase = bin_index[:, None] * lag_index[None, :] % SAMPLES
    lag_angles = lag_phase.astype(jnp.float32) * (2.0 * math.pi / SAMPLES)
    lag_table = jnp.concatenate(
        [jnp.cos(lag_angles).astype(jnp.bfloat16), (-jnp.sin(lag_angles)).astype(jnp.bfloat16)],
        axis=0,
    )
    lagged = jnp.dot(
        stacked.reshape(BLOCK * chan_rows, 2 * FBINS), lag_table, preferred_element_type=jnp.float32
    )
    lagged = lagged.reshape(BLOCK, chan_rows, LAGS)
    factor = 2.0 / (SAMPLES * math.sqrt(FBINS))
    return (lagged * factor / jnp.maximum(counts, 1.0)[:, :, None]).astype(jnp.bfloat16)


def solution(mesh):
    in_specs = (
        P(None, ("groups", "chan"), None),
        P(),
        P(("groups", "chan"), None),
        P(None, "groups"),
        P("groups"),
        P("groups"),
    )
    out_specs = P(None, ("groups", "chan"), None)
    return jax.shard_map(body, mesh=mesh, in_specs=in_specs, out_specs=out_specs, check_vma=False)
```

profile of v0, /device:TPU:0, one launch (start us, length us, event | category | flops | bytes accessed | tf_op | source)
XLA Modules:
  0.0 450.7 jit_solution(18336258818147631185)
XLA Ops:
  6.5 0.0 copy-start
  6.5 0.0 all-gather.2.cloned.1.call-start
  6.5 0.1 fusion.50
  6.6 0.1 fusion.55
  6.7 0.7 convert_element_type.83
  7.4 0.8 copy.13
  8.2 115.1 %gather_fusion = bf16[32768,16]{1,0:T(8,128)(2,1)} fusion(bf16[16,64]{0,1:T(8,128)(2,1)S(1)} %copy.13, s32[32768]{0:T(1024)S(1)} %fusion.50), kind=kCustom, calls=%fused_computation | custom fusion | bytes 2228224 | tf_op jit(solution)/shard_map/jit(_take)/gather | solution.py:20
  123.3 6.8 %copy.14 = bf16[256,128,16]{1,0,2:T(8,128)(2,1)S(1)} copy(bf16[256,128,16]{2,1,0:T(8,128)(2,1)} %bitcast.76) | data formatting | bytes 2097152 | tf_op jit(solution)/shard_map/jit(_take)/gather | solution.py:20
  130.1 0.0 copy-done
  130.1 0.0 copy-start.2
  130.1 191.6 %gather_fusion.1 = bf16[32768]{0:T(1024)(128)(2,1)S(1)} fusion(bf16[64]{0:T(256)(128)(2,1)S(1)} %copy-done, s32[32768]{0:T(1024)S(1)} %fusion.50), kind=kCustom, calls=%fused_computation.1 | custom fusion | bytes 262144 | tf_op jit(solution)/shard_map/jit(_take)/gather | solution.py:20
  321.7 0.0 copy-done.2
  321.7 0.2 copy.31
  322.0 0.1 slice.39
  322.1 0.9 multiply_reduce_fusion
  323.0 0.3 divide_convert_fusion.1
  323.2 0.1 slice.41
  323.3 0.8 fusion.32
  324.1 0.1 copy.16
  324.2 0.5 copy.49
  324.7 39.7 %while.16 = (s32[]{:T(128)}, f32[128,1024]{1,0:T(8,128)S(1)}, bf16[128,4096]{1,0:T(8,128)(2,1)S(1)}, s32[]{:T(128)}, s32[]{:T(128)}, /*index=5*/s32[]{:T(128)}, s32[]{:T(128)}) while((s32[]{:T(128)}, f32[128,1024]{1,0:T(8,128)S(1)}, bf16[128,4096]{1,0:T(8,128)(2,1)S(1)}, s32[]{:T(128)}, s32[]{:T(128)}, /*index=5*/s32[]{:T(128)}, ...), condition=%wide.region_2.3_spmd.clone, body=%wide.region_1.2_spmd.clone.sunk | while | flops 141034496 | bytes 3285141 | solution.py:61
  324.7 4.6 %cosine_convert_fusion.3 = (bf16[512,512]{1,0:T(8,128)(2,1)S(1)}, bf16[512,512]{1,0:T(8,128)(2,1)S(1)}) fusion(s32[512]{0:T(512)S(1)} %get-tuple-element.174, s32[512]{0:T(512)S(1)} %get-tuple-element.175), kind=kLoop, calls=%fused_computation.16.clone.1 | loop fusion | flops 4456448 | bytes 1052672 | tf_op jit(solution)/shard_map/while/body/eval_jaxpr/convert_element_type | solution.py:57
  329.3 0.3 convolution_add_fusion.2
  329.7 4.6 %cosine_convert_fusion.3 = (bf16[512,512]{1,0:T(8,128)(2,1)S(1)}, bf16[512,512]{1,0:T(8,128)(2,1)S(1)}) fusion(s32[512]{0:T(512)S(1)} %get-tuple-element.174, s32[512]{0:T(512)S(1)} %get-tuple-element.175), kind=kLoop, calls=%fused_computation.16.clone.1 | loop fusion | flops 4456448 | bytes 1052672 | tf_op jit(solution)/shard_map/while/body/eval_jaxpr/convert_element_type | solution.py:57
  334.3 0.3 convolution_add_fusion.2
  334.7 4.6 %cosine_convert_fusion.3 = (bf16[512,512]{1,0:T(8,128)(2,1)S(1)}, bf16[512,512]{1,0:T(8,128)(2,1)S(1)}) fusion(s32[512]{0:T(512)S(1)} %get-tuple-element.174, s32[512]{0:T(512)S(1)} %get-tuple-element.175), kind=kLoop, calls=%fused_computation.16.clone.1 | loop fusion | flops 4456448 | bytes 1052672 | tf_op jit(solution)/shard_map/while/body/eval_jaxpr/convert_element_type | solution.py:57
  339.3 0.3 convolution_add_fusion.2
  339.6 4.6 %cosine_convert_fusion.3 = (bf16[512,512]{1,0:T(8,128)(2,1)S(1)}, bf16[512,512]{1,0:T(8,128)(2,1)S(1)}) fusion(s32[512]{0:T(512)S(1)} %get-tuple-element.174, s32[512]{0:T(512)S(1)} %get-tuple-element.175), kind=kLoop, calls=%fused_computation.16.clone.1 | loop fusion | flops 4456448 | bytes 1052672 | tf_op jit(solution)/shard_map/while/body/eval_jaxpr/convert_element_type | solution.py:57
  344.2 0.3 convolution_add_fusion.2
  344.6 4.6 %cosine_convert_fusion.3 = (bf16[512,512]{1,0:T(8,128)(2,1)S(1)}, bf16[512,512]{1,0:T(8,128)(2,1)S(1)}) fusion(s32[512]{0:T(512)S(1)} %get-tuple-element.174, s32[512]{0:T(512)S(1)} %get-tuple-element.175), kind=kLoop, calls=%fused_computation.16.clone.1 | loop fusion | flops 4456448 | bytes 1052672 | tf_op jit(solution)/shard_map/while/body/eval_jaxpr/convert_element_type | solution.py:57
  349.2 0.3 convolution_add_fusion.2
  349.6 4.6 %cosine_convert_fusion.3 = (bf16[512,512]{1,0:T(8,128)(2,1)S(1)}, bf16[512,512]{1,0:T(8,128)(2,1)S(1)}) fusion(s32[512]{0:T(512)S(1)} %get-tuple-element.174, s32[512]{0:T(512)S(1)} %get-tuple-element.175), kind=kLoop, calls=%fused_computation.16.clone.1 | loop fusion | flops 4456448 | bytes 1052672 | tf_op jit(solution)/shard_map/while/body/eval_jaxpr/convert_element_type | solution.py:57
  354.2 0.3 convolution_add_fusion.2
  354.5 4.6 %cosine_convert_fusion.3 = (bf16[512,512]{1,0:T(8,128)(2,1)S(1)}, bf16[512,512]{1,0:T(8,128)(2,1)S(1)}) fusion(s32[512]{0:T(512)S(1)} %get-tuple-element.174, s32[512]{0:T(512)S(1)} %get-tuple-element.175), kind=kLoop, calls=%fused_computation.16.clone.1 | loop fusion | flops 4456448 | bytes 1052672 | tf_op jit(solution)/shard_map/while/body/eval_jaxpr/convert_element_type | solution.py:57
  359.1 0.3 convolution_add_fusion.2
  359.5 4.6 %cosine_convert_fusion.3 = (bf16[512,512]{1,0:T(8,128)(2,1)S(1)}, bf16[512,512]{1,0:T(8,128)(2,1)S(1)}) fusion(s32[512]{0:T(512)S(1)} %get-tuple-element.174, s32[512]{0:T(512)S(1)} %get-tuple-element.175), kind=kLoop, calls=%fused_computation.16.clone.1 | loop fusion | flops 4456448 | bytes 1052672 | tf_op jit(solution)/shard_map/while/body/eval_jaxpr/convert_element_type | solution.py:57
  364.1 0.3 convolution_add_fusion.2
  364.4 0.0 copy-start.4
  364.5 0.4 reshape.130
  364.9 0.1 constant_dynamic-slice_fusion
  365.0 0.0 copy-start.3
  365.0 0.9 fusion.46
  365.8 0.0 all-gather.2.cloned.1.call-update
  366.5 0.0 copy-done.4
  366.5 0.3 reduce-window.9
  366.9 0.1 slice.31
  367.0 0.2 fusion.90
  367.1 2.0 copy.26
  369.1 0.1 slice_reduce_fusion
  369.2 0.1 add_bitcast_fusion
  369.3 0.0 copy-done.3
  369.3 0.3 fusion.38
  369.6 9.7 %cosine_convert_fusion.1 = (bf16[512,1024]{1,0:T(8,128)(2,1)S(1)}, bf16[512,1024]{1,0:T(8,128)(2,1)}) fusion(s32[1024]{0:T(1024)S(1)} %iota_add_fusion.2, s32[512]{0:T(512)S(1)} %iota_add_fusion.3), kind=kLoop, calls=%fused_computation.50 | loop fusion | flops 8912896 | bytes 2103296 | tf_op jit(solution)/shard_map/convert_element_type | solution.py:87
  379.3 40.2 %all-gather.2.cloned.1.call-done = bf16[8,256,2,512]{3,1,2,0:T(8,128)(2,1)} async-done(((bf16[8,16,2,512]{3,1,2,0:T(8,128)(2,1)}), bf16[8,256,2,512]{3,1,2,0:T(8,128)(2,1)}) %all-gather.2.cloned.1.call-update) | async-done | bytes 4194320 | tf_op jit(solution)/shard_map/all_gather | solution.py:79
  419.5 3.5 convolution_convert_fusion
  423.0 0.2 slice_negate_fusion
  423.2 0.2 maximum_bitcast_fusion
  423.4 0.4 pad_maximum_fusion
  423.8 9.2 %fusion.11 = bf16[128,16,2,512]{0,1,2,3:T(8,128)(2,1)S(1)} fusion(bf16[8,16,2,512,1]{1,0,2,4,3:T(8,128)(2,1)S(1)} %copy.26, bf16[2,8,128,2,512]{2,4,3,1,0:T(8,128)(2,1)S(1)} %pad_maximum_fusion), kind=kOutput, calls=%fused_computation.24 | convolution fusion | flops 69206016 | bytes 8650752 | tf_op jit(solution)/shard_map/jgskf,grkf->srjf/dot_general | solution.py:34
  433.0 0.0 copy-start.1
  433.0 1.6 copy.20
  434.7 0.0 copy-done.1
  434.7 4.8 %divide_convert_fusion = bf16[128,16,1024]{2,0,1:T(8,128)(2,1)S(1)} fusion(f32[128,16]{0,1:T(8,128)S(1)} %fusion.38, bf16[128,16,1024]{0,2,1:T(8,128)(2,1)S(1)} %bitcast.77, bf16[512,1024]{1,0:T(8,128)(2,1)S(1)} %copy-done.1, bf16[512,1024]{1,0:T(8,128)(2,1)S(1)} %get-tuple-element.145), kind=kOutput, calls=%fused_computation.23 | convolution fusion | flops 4305453056 | bytes 10493952 | tf_op jit(solution)/shard_map/dot_general | solution.py:90
  439.5 4.3 copy.22
  (15 shorter events, 0.1 us)
Async XLA Ops:
  6.5 123.6 %copy-start = (bf16[64]{0:T(256)(128)(2,1)S(1)}, bf16[64]{0:T(256)(128)(2,1)}, u32[]{:S(2)}) copy-start(bf16[64]{0:T(256)(128)(2,1)} %param.9) | copy-start | bytes 388
  6.5 413.0 %all-gather.2.cloned.1.call-start = ((), (), s32[]{:S(2)}) async-start(), calls=%async_computation | async-start | bytes 4456448 | tf_op jit(solution)/shard_map/all_gather | solution.py:79
  130.1 191.6 %copy-start.2 = (bf16[8,16,4096]{2,1,0:T(8,128)(2,1)S(1)}, bf16[8,16,4096]{2,1,0:T(8,128)(2,1)}, u32[]{:S(2)}) copy-start(bf16[8,16,4096]{2,1,0:T(8,128)(2,1)} %param.8) | copy-start | bytes 3145732
  364.4 2.1 copy-start.4
  365.0 4.3 copy-start.3
  433.0 1.6 copy-start.1
Sparse Core Ops, SparseCore 0:
  366.0 53.4 all-gather.1
where the time goes:
time: 451 us
  local copies, waits for them, and re-layouts  324 us (72%)
  other arithmetic  49.7 us (11%)
  waiting for transfers between devices  40.3 us (9%)
  matrix products  22.2 us (5%)
  between operations  14.3 us (3%)
    gather x3, local copies, waits for them, and re-layouts, fir_matrix(): jnp.take(coeffs, jnp.clip(offset, 0, coeffs.shape[-1] - 1), axis=-1)  313 us
    all_gather x1, waiting for transfers between devices, body(): lax.all_gather(spectra, 'chan', axis=1, tiled=True)  40.2 us
    convert_element_type x8, other arithmetic, add_block(): jnp.cos(angles).astype(jnp.bfloat16)  36.6 us
    convert_element_type x1, other arithmetic, body(): jnp.cos(lag_angles).astype(jnp.bfloat16)  9.69 us
    dot_general x1, matrix products, cross_stack(): jnp.einsum('jgskf,grkf->srjf', paired, receivers, preferred_element_type=...  9.21 us
  transfers between devices with their start and end apart: 1, of which 1 were waited for; matrix products, arithmetic and copies ran while one was open for 3% of the time, Pallas kernels for 0%

commit v1 on v0

--- a/solution.py
+++ b/solution.py
@@ -1,6 +1,7 @@
 import math
 
 import jax
+import numpy as np
 import jax.numpy as jnp
 from jax import lax
 from jax.sharding import PartitionSpec as P
@@ -10,6 +11,21 @@
 FBINS = 512
 LAGS = 1024
 BLOCK = 128
+
+
+def table(phase):
+    angles = phase.astype(np.float32) * np.float32(2.0 * math.pi / SAMPLES)
+    return np.cos(angles).astype(jnp.bfloat16), (-np.sin(angles)).astype(jnp.bfloat16)
+
+
+def dft_table():
+    bins = KLO + np.arange(FBINS)
+    return np.concatenate(table(np.arange(SAMPLES)[:, None] * bins[None, :] % SAMPLES), axis=1)
+
+
+def lag_table_np():
+    bins = KLO + np.arange(FBINS)
+    return np.concatenate(table(bins[:, None] * (np.arange(LAGS) - LAGS // 2)[None, :] % SAMPLES), axis=0)
 
 
 def fir_matrix(coeffs):
@@ -44,31 +60,14 @@
     normalized = (filtered / jnp.sqrt(energy + 1e-05)).astype(jnp.bfloat16)
     whitened = fir_pass(normalized, fir_matrix(whiten_taps), "gcbi,cio->gcbo").astype(jnp.bfloat16)
     time_rows = whitened.reshape(seg_count * chan_rows, sample_count)
-    block_width = min(512, sample_count)
-    bin_index = KLO + jnp.arange(FBINS, dtype=jnp.int32)
-
-    def add_block(step_index, running):
-        first_time = step_index * block_width
-        piece_rows = lax.dynamic_slice_in_dim(time_rows, first_time, block_width, 1)
-        sample_idx = first_time + jnp.arange(block_width, dtype=jnp.int32)
-        phase_idx = sample_idx[:, None] * bin_index[None, :] % SAMPLES
-        angles = phase_idx.astype(jnp.float32) * (2.0 * math.pi / SAMPLES)
-        dft_table = jnp.concatenate(
-            [jnp.cos(angles).astype(jnp.bfloat16), (-jnp.sin(angles)).astype(jnp.bfloat16)], axis=1
-        )
-        return running + jnp.dot(piece_rows, dft_table, preferred_element_type=jnp.float32)
-
-    spectra = lax.fori_loop(
-        0,
-        sample_count // block_width,
-        add_block,
-        jnp.zeros((seg_count * chan_rows, 2 * FBINS), jnp.float32),
-    )
+    spectra = jnp.dot(time_rows, jnp.asarray(dft_table()), preferred_element_type=jnp.float32)
     spectra = (
         spectra.reshape(seg_count, chan_rows, 2, FBINS) * mask_here[:, :, None, None]
     ).astype(jnp.bfloat16)
     member = channel_block == source_block[0]
-    member_rank = jnp.cumsum(member.astype(jnp.int32)) - 1
+    order = jnp.arange(member.shape[0], dtype=jnp.int32)
+    below = member[None, :] & (order[None, :] < order[:, None])
+    member_rank = jnp.sum(below.astype(jnp.int32), axis=1)
     chosen = member[None, :] & (member_rank[None, :] == jnp.arange(BLOCK, dtype=jnp.int32)[:, None])
     selector = chosen.astype(jnp.bfloat16)
     source_mask = jnp.dot(mask_all, chosen.astype(jnp.float32).T)
@@ -80,13 +79,7 @@
         preferred_element_type=jnp.float32,
     ).astype(jnp.bfloat16)
     stacked = cross_stack(sources, spectra).astype(jnp.bfloat16)
-    lag_index = jnp.arange(LAGS, dtype=jnp.int32) - LAGS // 2
-    lag_phase = bin_index[:, None] * lag_index[None, :] % SAMPLES
-    lag_angles = lag_phase.astype(jnp.float32) * (2.0 * math.pi / SAMPLES)
-    lag_table = jnp.concatenate(
-        [jnp.cos(lag_angles).astype(jnp.bfloat16), (-jnp.sin(lag_angles)).astype(jnp.bfloat16)],
-        axis=0,
-    )
+    lag_table = jnp.asarray(lag_table_np())
     lagged = jnp.dot(
         stacked.reshape(BLOCK * chan_rows, 2 * FBINS), lag_table, preferred_element_type=jnp.float32
     )

time: 451 us -> 416 us (0.922)
  other arithmetic: 49.7 us -> 2.04 us
  waiting for transfers between devices: 40.3 us -> 49.5 us
    convert_element_type x11 -> x0, other arithmetic: 47.4 us -> none  [the longest x8 36.6 us: add_block(): jnp.cos(angles).astype(jnp.bfloat16)]
    all_gather x1, waiting for transfers between devices: 40.2 us -> 49.5 us  [body(): lax.all_gather(spectra, 'chan', axis=1, tiled=True)]
  transfers between devices with their start and end apart: 1 -> 1, of which waited for: 1 -> 1; matrix products, arithmetic and copies ran while one was open for 3% -> 1% of each run, Pallas kernels for 0% -> 0%
where the time goes in v1:
time: 416 us
  local copies, waits for them, and re-layouts  323 us (78%)
  waiting for transfers between devices  49.5 us (12%)
  matrix products  26.6 us (6%)
  between operations  14.2 us (3%)
    gather x3, local copies, waits for them, and re-layouts, fir_matrix(): jnp.take(coeffs, jnp.clip(offset, 0, coeffs.shape[-1] - 1), axis=-1)  313 us
    all_gather x1, waiting for transfers between devices, body(): lax.all_gather(spectra, 'chan', axis=1, tiled=True)  49.5 us
    dot_general x1, matrix products, cross_stack(): jnp.einsum('jgskf,grkf->srjf', paired, receivers, preferred_element_type=...  9.21 us
  transfers between devices with their start and end apart: 1, of which 1 were waited for; matrix products, arithmetic and copies ran while one was open for 1% of the time, Pallas kernels for 0%

profile of v1, /device:TPU:0, one launch (start us, length us, event | category | flops | bytes accessed | tf_op | source)
XLA Modules:
  0.0 415.6 jit_solution(9647305675959795100)
XLA Ops:
  6.5 0.0 copy-start
  6.5 0.0 all-gather.2.cloned.1.call-start
  6.5 0.1 fusion.32
  6.6 0.1 fusion.37
  6.7 0.7 convert_element_type.45
  7.4 0.8 copy.25
  8.2 114.3 %gather_fusion = bf16[32768,16]{1,0:T(8,128)(2,1)} fusion(bf16[16,64]{0,1:T(8,128)(2,1)S(1)} %copy.25, s32[32768]{0:T(1024)S(1)} %fusion.32), kind=kCustom, calls=%fused_computation | custom fusion | bytes 2228224 | tf_op jit(solution)/shard_map/jit(_take)/gather | solution.py:36
  122.5 6.8 %copy.26 = bf16[256,128,16]{1,0,2:T(8,128)(2,1)S(1)} copy(bf16[256,128,16]{2,1,0:T(8,128)(2,1)} %bitcast.72) | data formatting | bytes 2097152 | tf_op jit(solution)/shard_map/jit(_take)/gather | solution.py:36
  129.3 0.0 copy-done
  129.3 0.0 copy-start.1
  129.3 191.6 %gather_fusion.1 = bf16[32768]{0:T(1024)(128)(2,1)S(1)} fusion(bf16[64]{0:T(256)(128)(2,1)S(1)} %copy-done, s32[32768]{0:T(1024)S(1)} %fusion.32), kind=kCustom, calls=%fused_computation.1 | custom fusion | bytes 262144 | tf_op jit(solution)/shard_map/jit(_take)/gather | solution.py:36
  320.9 0.0 copy-done.1
  320.9 0.2 copy.45
  321.2 0.1 slice.30
  321.3 0.9 multiply_reduce_fusion
  322.2 0.3 divide_convert_fusion.1
  322.4 0.1 slice.32
  322.5 0.8 fusion.16
  323.4 0.5 convert_element_type.44
  323.9 0.1 constant_dynamic-slice_fusion
  323.9 0.0 copy-start.3
  323.9 0.0 copy-start.2
  323.9 7.0 %fusion.19 = bf16[8,16,2,512]{3,1,2,0:T(8,128)(2,1)} fusion(bf16[2,512,4096,1]{2,1,0,3:T(8,128)(2,1)} %constant.67, bf16[8,16,4096,1]{2,0,1,3:T(8,128)(2,1)S(1)} %bitcast.80, f32[8,16]{1,0:T(8,128)S(1)} %constant_dynamic-slice_fusion), kind=kOutput, calls=%fused_computation.24 | convolution fusion | flops 1074003968 | bytes 9699840 | tf_op jit(solution)/shard_map/dot_general | solution.py:63
  331.0 0.0 all-gather.2.cloned.1.call-update
  331.6 2.8 copy.38
  334.5 0.0 copy-done.3
  334.5 0.1 convert_reduce_fusion
  334.6 0.0 copy-done.2
  334.6 0.3 convolution_maximum_fusion
  334.9 49.5 %all-gather.2.cloned.1.call-done = bf16[8,256,2,512]{3,1,2,0:T(8,128)(2,1)} async-done(((bf16[8,16,2,512]{3,1,2,0:T(8,128)(2,1)}), bf16[8,256,2,512]{3,1,2,0:T(8,128)(2,1)}) %all-gather.2.cloned.1.call-update) | async-done | bytes 4194320 | tf_op jit(solution)/shard_map/all_gather | solution.py:78
  384.4 3.5 convolution_convert_fusion
  387.9 0.2 slice_negate_fusion
  388.1 0.2 maximum_bitcast_fusion
  388.3 0.4 pad_maximum_fusion
  388.7 9.2 %fusion = bf16[128,16,2,512]{0,1,2,3:T(8,128)(2,1)S(1)} fusion(bf16[8,16,2,512,1]{1,0,2,4,3:T(8,128)(2,1)S(1)} %copy.38, bf16[2,8,128,2,512]{2,4,3,1,0:T(8,128)(2,1)S(1)} %pad_maximum_fusion), kind=kOutput, calls=%fused_computation.4 | convolution fusion | flops 69206016 | bytes 8650752 | tf_op jit(solution)/shard_map/jgskf,grkf->srjf/dot_general | solution.py:50
  398.0 0.0 copy-start.4
  398.0 1.6 copy.31
  399.6 0.0 copy-done.4
  399.6 4.8 %divide_convert_fusion = bf16[128,16,1024]{2,0,1:T(8,128)(2,1)S(1)} fusion(f32[128,16]{0,1:T(8,128)S(1)} %convolution_maximum_fusion, bf16[128,16,1024]{0,2,1:T(8,128)(2,1)S(1)} %bitcast.73, bf16[1024,1024,1]{1,0,2:T(8,128)(2,1)S(1)} %copy-done.4), kind=kOutput, calls=%fused_computation.3 | convolution fusion | flops 4301258752 | bytes 10493952 | tf_op jit(solution)/shard_map/dot_general | solution.py:83
  404.5 4.3 %copy.33 = bf16[128,16,1024]{2,1,0:T(8,128)(2,1)} copy(bf16[128,16,1024]{2,0,1:T(8,128)(2,1)S(1)} %divide_convert_fusion) | data formatting | bytes 8388608 | tf_op jit(solution)/shard_map/convert_element_type | solution.py:88
  (3 shorter events, 0.0 us)
Async XLA Ops:
  6.5 122.8 %copy-start = (bf16[64]{0:T(256)(128)(2,1)S(1)}, bf16[64]{0:T(256)(128)(2,1)}, u32[]{:S(2)}) copy-start(bf16[64]{0:T(256)(128)(2,1)} %param.9) | copy-start | bytes 388
  6.5 377.9 %all-gather.2.cloned.1.call-start = ((), (), s32[]{:S(2)}) async-start(), calls=%async_computation | async-start | bytes 4456448 | tf_op jit(solution)/shard_map/all_gather | solution.py:78
  129.3 191.6 %copy-start.1 = (bf16[8,16,4096]{2,1,0:T(8,128)(2,1)S(1)}, bf16[8,16,4096]{2,1,0:T(8,128)(2,1)}, u32[]{:S(2)}) copy-start(bf16[8,16,4096]{2,1,0:T(8,128)(2,1)} %param.8) | copy-start | bytes 3145732
  323.9 10.6 %copy-start.3 = (s32[256]{0:T(256)S(1)}, s32[256]{0:T(256)}, u32[]{:S(2)}) copy-start(s32[256]{0:T(256)} %param.12) | copy-start | bytes 3076
  323.9 10.7 %copy-start.2 = (s32[8,256]{1,0:T(8,128)S(1)}, s32[8,256]{1,0:T(8,128)}, u32[]{:S(2)}) copy-start(s32[8,256]{1,0:T(8,128)} %param.11) | copy-start | bytes 24580
  398.0 1.6 copy-start.4
Sparse Core Ops, SparseCore 0:
  331.1 53.2 all-gather.1

commit v2 on v1

v2 whole, which is shorter than its diff:
```python
import math

import jax
import numpy as np
import jax.numpy as jnp
from jax import lax
from jax.experimental import pallas as pl
from jax.experimental.pallas import tpu as pltpu
from jax.sharding import PartitionSpec as P

SAMPLES = 4096
KLO = 64
FBINS = 512
LAGS = 1024
BLOCK = 128


def table(phase):
    angles = phase.astype(np.float32) * np.float32(2.0 * math.pi / SAMPLES)
    return np.cos(angles).astype(jnp.bfloat16), (-np.sin(angles)).astype(jnp.bfloat16)


def dft_table():
    bins = KLO + np.arange(FBINS)
    return np.concatenate(table(np.arange(SAMPLES)[:, None] * bins[None, :] % SAMPLES), axis=1)


def lag_table_np():
    bins = KLO + np.arange(FBINS)
    return np.concatenate(table(bins[:, None] * (np.arange(LAGS) - LAGS // 2)[None, :] % SAMPLES), axis=0)


def toeplitz(taps):
    turned = pltpu.roll(jnp.broadcast_to(taps, (128, 128)), 0, 1, stride=1, stride_axis=0)
    row = lax.broadcasted_iota(jnp.int32, (128, 128), 0)
    lane = lax.broadcasted_iota(jnp.int32, (128, 128), 1)
    before = jnp.where(lane < row, turned, 0.0)
    here = jnp.where(lane >= row, turned, 0.0)
    return jnp.concatenate([before, here], axis=0).astype(jnp.bfloat16)


def front_kernel(raw_ref, band_ref, taps_ref, mask_ref, table_ref, out_ref, filt, inv, white, acc):
    segs, rows, samples = raw_ref.shape
    blocks = samples // 128
    step = pl.program_id(0)
    depth = table_ref.shape[0]

    @pl.when(step == 0)
    def _():
        matrix = toeplitz(band_ref[...])
        power = jnp.zeros((segs * rows, 128), jnp.float32)
        for b in range(blocks):
            if b == 0:
                joined = jnp.concatenate([raw_ref[:, :, samples - 128 :], raw_ref[:, :, :128]], axis=2)
            else:
                joined = raw_ref[:, :, (b - 1) * 128 : (b + 1) * 128]
            part = jnp.dot(joined.reshape(segs * rows, 256), matrix, preferred_element_type=jnp.float32)
            power = power + part * part
            filt[:, :, b * 128 : (b + 1) * 128] = part.reshape(segs, rows, 128)
        energy = jnp.sum(power, axis=1, keepdims=True) * (1.0 / samples)
        scale = 1.0 / jnp.sqrt(energy + 1e-05)
        inv[...] = jnp.broadcast_to(scale, (segs * rows, 128)).reshape(segs, rows, 128)
        for c in range(rows):
            matrix = toeplitz(taps_ref[c : c + 1, :])
            scale = inv[:, c, :]
            here = jnp.concatenate(
                [filt[:, c, b * 128 : (b + 1) * 128] * scale for b in range(blocks)], axis=0
            )
            before = jnp.concatenate([here[-segs:], here[:-segs]], axis=0)
            joined = jnp.concatenate([before, here], axis=1).astype(jnp.bfloat16)
            part = jnp.dot(joined, matrix, preferred_element_type=jnp.float32)
            for b in range(blocks):
                white[c * segs : (c + 1) * segs, b * 128 : (b + 1) * 128] = part[b * segs : (b + 1) * segs]
        acc[...] = jnp.zeros_like(acc)

    first = pl.multiple_of(step * depth, depth)
    acc[...] += jnp.dot(
        white[:, pl.ds(first, depth)].astype(jnp.bfloat16), table_ref[...], preferred_element_type=jnp.float32
    )

    @pl.when(step == pl.num_programs(0) - 1)
    def _():
        out_ref[...] = (acc[...] * mask_ref[...]).astype(jnp.bfloat16)


def front(raw, bandpass, whiten_taps, mask_here):
    segs, rows, samples = raw.shape
    pad = ((0, 0), (0, 128 - bandpass.shape[-1]))
    band = jnp.pad(bandpass.astype(jnp.float32)[None], pad)
    taps = jnp.pad(whiten_taps.astype(jnp.float32), pad)
    mask = mask_here.T.reshape(rows * segs, 1)
    depth = 512
    whole = lambda *shape: pl.BlockSpec(shape, lambda i: (0,) * len(shape))
    return pl.pallas_call(
        front_kernel,
        grid=(samples // depth,),
        out_shape=jax.ShapeDtypeStruct((rows * segs, 2 * FBINS), jnp.bfloat16),
        in_specs=[
            whole(segs, rows, samples),
            whole(1, 128),
            whole(rows, 128),
            whole(rows * segs, 1),
            pl.BlockSpec((depth, 2 * FBINS), lambda i: (i, 0)),
        ],
        out_specs=whole(rows * segs, 2 * FBINS),
        scratch_shapes=[
            pltpu.VMEM((segs, rows, samples), jnp.float32),
            pltpu.VMEM((segs, rows, 128), jnp.float32),
            pltpu.VMEM((rows * segs, samples), jnp.float32),
            pltpu.VMEM((rows * segs, 2 * FBINS), jnp.float32),
        ],
        compiler_params=pltpu.CompilerParams(vmem_limit_bytes=40 * 2**20),
        cost_estimate=pl.CostEstimate(flops=2 * 10**9, bytes_accessed=10**7, transcendentals=0),
    )(raw, band, taps, mask, jnp.asarray(dft_table()))


def cross_stack(sources, receivers):
    turned = jnp.stack([-sources[:, :, 1], sources[:, :, 0]], axis=2)
    paired = jnp.stack([sources, turned], axis=0)
    return jnp.einsum("jsgkf,rgkf->srjf", paired, receivers, preferred_element_type=jnp.float32)


def body(raw_strain, bandpass, whiten_taps, segment_mask, channel_block, source_block):
    seg_count, chan_rows, sample_count = raw_strain.shape
    chan_start = lax.axis_index("chan") * chan_rows
    mask_all = segment_mask.astype(jnp.float32)
    mask_here = lax.dynamic_slice_in_dim(mask_all, chan_start, chan_rows, 1)
    spectra = front(raw_strain, bandpass, whiten_taps, mask_here)
    gathered = lax.all_gather(spectra, "chan", axis=0, tiled=True).reshape(-1, seg_count, 2, FBINS)
    spectra = spectra.reshape(chan_rows, seg_count, 2, FBINS)
    member = channel_block == source_block[0]
    order = jnp.arange(member.shape[0], dtype=jnp.int32)
    below = member[None, :] & (order[None, :] < order[:, None])
    member_rank = jnp.sum(below.astype(jnp.int32), axis=1)
    chosen = member[None, :] & (member_rank[None, :] == jnp.arange(BLOCK, dtype=jnp.int32)[:, None])
    selector = chosen.astype(jnp.bfloat16)
    source_mask = jnp.dot(mask_all, chosen.astype(jnp.float32).T)
    counts = jnp.dot(source_mask.T, mask_here)
    sources = jnp.einsum(
        "sc,cgkf->sgkf",
        selector,
        gathered,
        preferred_element_type=jnp.float32,
    ).astype(jnp.bfloat16)
    stacked = cross_stack(sources, spectra).astype(jnp.bfloat16)
    lag_table = jnp.asarray(lag_table_np())
    lagged = jnp.dot(
        stacked.reshape(BLOCK * chan_rows, 2 * FBINS), lag_table, preferred_element_type=jnp.float32
    )
    lagged = lagged.reshape(BLOCK, chan_rows, LAGS)
    factor = 2.0 / (SAMPLES * math.sqrt(FBINS))
    return (lagged * factor / jnp.maximum(counts, 1.0)[:, :, None]).astype(jnp.bfloat16)


def solution(mesh):
    in_specs = (
        P(None, ("groups", "chan"), None),
        P(),
        P(("groups", "chan"), None),
        P(None, "groups"),
        P("groups"),
        P("groups"),
    )
    out_specs = P(None, ("groups", "chan"), None)
    return jax.shard_map(body, mesh=mesh, in_specs=in_specs, out_specs=out_specs, check_vma=False)
```

time: 416 us -> 113 us (0.27)
  local copies, waits for them, and re-layouts: 323 us -> 22.3 us
  matrix products: 26.6 us -> 15.7 us
  Pallas kernels: 0 us -> 6.5 us
    gather x3 -> x0, local copies, waits for them, and re-layouts: 313 us -> none  [fir_matrix(): jnp.take(coeffs, jnp.clip(offset, 0, coeffs.shape[-1] - 1), axis=-1)]
    dot_general x5 -> x2, matrix products: 21.4 us -> 10.6 us  [the longest x1 7.08 us: body(): jnp.einsum('sc,cgkf->sgkf', selector, gathered, preferred_element_type=jn...]
    another operation x0 -> x1, local copies, waits for them, and re-layouts: none -> 7.86 us  [cross_stack(): paired = jnp.stack([sources, turned], axis=0)]
    pallas_call x0 -> x1, Pallas kernels: none -> 6.5 us  [front(): pl.pallas_call(front_kernel, grid=(samples // depth,), out_shape=jax.Shap...]
  transfers between devices with their start and end apart: 1 -> 1, of which waited for: 1 -> 1; matrix products, arithmetic and copies ran while one was open for 1% -> 4% of each run, Pallas kernels for 0% -> 0%
where the time goes in v2:
time: 113 us; the launch traced here: 112 us
  waiting for transfers between devices  48.7 us (43%)
  local copies, waits for them, and re-layouts  22.3 us (20%)
  matrix products  15.7 us (14%)
  between operations  14.1 us (12%)
  Pallas kernels  6.5 us (6%)
  other arithmetic  4.88 us (4%)
    all_gather x1, waiting for transfers between devices, body(): lax.all_gather(spectra, 'chan', axis=0, tiled=True)  48.7 us
    another operation x1, local copies, waits for them, and re-layouts, cross_stack(): paired = jnp.stack([sources, turned], axis=0)  7.86 us
    dot_general x1, matrix products, body(): jnp.einsum('sc,cgkf->sgkf', selector, gathered, preferred_element_type=jn...  7.08 us
    pallas_call x1, Pallas kernels, front(): pl.pallas_call(front_kernel, grid=(samples // depth,), out_shape=jax.Shap...  6.5 us
    dot_general x1, matrix products, body(): jnp.dot(stacked.reshape(BLOCK * chan_rows, 2 * FBINS), lag_table, preferr...  4.88 us
    unnamed x8, local copies, waits for them, and re-layouts  4.61 us
    convert_element_type x1, local copies, waits for them, and re-layouts, body(): (lagged * factor / jnp.maximum(counts, 1.0)[:, :, None]).astype(jnp.bfloa...  4.34 us
    reshape x1, local copies, waits for them, and re-layouts, body(): spectra = spectra.reshape(chan_rows, seg_count, 2, FBINS)  3.63 us
  transfers between devices with their start and end apart: 1, of which 1 were waited for; matrix products, arithmetic and copies ran while one was open for 4% of the time, Pallas kernels for 0%

profile of v2, /device:TPU:0, one launch (start us, length us, event | category | flops | bytes accessed | tf_op | source)
XLA Modules:
  0.0 112.3 jit_solution(7321262382907164212)
XLA Ops:
  6.5 0.0 all-gather.2.cloned.1.call-start
  6.5 0.7 pad_convert_fusion.1.band_ref
  7.2 0.7 convert_element_type.26
  7.9 0.1 dynamic-slice_bitcast_fusion
  8.0 0.1 copy.23
  8.0 0.7 pad_convert_fusion.taps_ref
  8.7 0.1 reshape.23.mask_ref
  8.8 0.0 copy-start
  8.8 3.4 %copy-done = bf16[4096,1024]{1,0:T(8,128)(2,1)S(1)} copy-done((bf16[4096,1024]{1,0:T(8,128)(2,1)S(1)}, bf16[4096,1024]{1,0:T(8,128)(2,1)}, u32[]{:S(2)}) %copy-start) | copy-done | bytes 8388632
  12.2 0.0 copy-start.1
  12.2 1.2 %copy-done.1 = bf16[8,16,4096]{2,1,0:T(8,128)(2,1)S(1)} copy-done((bf16[8,16,4096]{2,1,0:T(8,128)(2,1)S(1)}, bf16[8,16,4096]{2,1,0:T(8,128)(2,1)}, u32[]{:S(2)}) %copy-start.1) | copy-done | bytes 1048600
  13.4 0.0 copy-start.2
  13.4 6.5 %shard_map.82 = bf16[128,1024]{1,0:T(8,128)(2,1)} custom-call(bf16[8,16,4096]{2,1,0:T(8,128)(2,1)S(1)} %copy-done.1, f32[1,128]{1,0:T(1,128)S(1)} %pad_convert_fusion.1.band_ref, f32[16,128]{1,0:T(8,128)S(1)} %pad_convert_fusion.taps_ref, f32[128,1]{1,0:T(8,128)S(1)} %reshape.23.mask_ref, bf16[4096,1024]{1,0:T(8,128)(2,1)S(1)} %copy-done), custom_call_target="tpu_custom_call" | custom-call | flops 2000000000 | bytes 10000000 | tf_op jit(solution)/shard_map/pallas_call | solution.py:94
  19.9 0.0 all-gather.2.cloned.1.call-update
  20.6 3.6 %copy.32 = bf16[16,8,2,512,1]{0,1,2,4,3:T(8,128)(2,1)S(1)} copy(bf16[16,8,2,512,1]{3,1,2,0,4:T(8,128)(2,1)} %bitcast.3) | data formatting | bytes 524288 | tf_op jit(solution)/shard_map/reshape | solution.py:130
  24.2 0.0 copy-done.2
  24.3 0.1 convert_reduce_fusion
  24.4 0.3 convolution_maximum_fusion
  24.7 48.7 %all-gather.2.cloned.1.call-done = bf16[2048,1024]{1,0:T(8,128)(2,1)} async-done(((bf16[128,1024]{1,0:T(8,128)(2,1)}), bf16[2048,1024]{1,0:T(8,128)(2,1)}) %all-gather.2.cloned.1.call-update) | async-done | bytes 4194320 | tf_op jit(solution)/shard_map/all_gather | solution.py:129
  73.4 7.1 %fusion.3 = bf16[128,8,2,512]{3,0,2,1:T(8,128)(2,1)S(1)} fusion(bf16[256,8,2,512]{3,1,2,0:T(8,128)(2,1)} %bitcast.32, s32[256]{0:T(256)S(1)} %convert_reduce_fusion, pred[256]{0:T(512)(128)(4,1)S(1)} %broadcast_compare_fusion), kind=kOutput, calls=%fused_computation.7 | convolution fusion | flops 537985024 | bytes 6292736 | tf_op jit(solution)/shard_map/sc,cgkf->sgkf/dot_general | solution.py:139
  80.5 0.1 slice_negate_fusion
  80.6 0.2 maximum_bitcast_fusion
  80.8 2.4 %pad_maximum_fusion = bf16[2,128,8,2,512]{4,1,3,2,0:T(8,128)(2,1)} fusion(bf16[1,128,8,2,512]{4,1,3,2,0:T(8,128)(2,1)S(1)} %maximum_bitcast_fusion, bf16[1,128,8,2,512]{4,1,3,2,0:T(8,128)(2,1)S(1)} %bitcast.31), kind=kLoop, calls=%fused_computation.3 | loop fusion | flops 2097152 | bytes 8388608 | tf_op jit(solution)/shard_map/stack | solution.py:119
  83.2 7.9 %copy.27 = bf16[2,128,8,2,512]{1,2,3,0,4:T(8,128)(2,1)} copy(bf16[2,128,8,2,512]{4,1,3,2,0:T(8,128)(2,1)} %pad_maximum_fusion) | data formatting | bytes 8388608 | tf_op jit(solution)/shard_map/stack | solution.py:119
  91.0 3.5 %fusion = bf16[128,16,2,512]{0,1,2,3:T(8,128)(2,1)S(1)} fusion(bf16[16,8,2,512,1]{0,1,2,4,3:T(8,128)(2,1)S(1)} %copy.32, bf16[2,128,8,2,512]{1,2,3,0,4:T(8,128)(2,1)} %copy.27), kind=kOutput, calls=%fused_computation.2 | convolution fusion | flops 69206016 | bytes 8650752 | tf_op jit(solution)/shard_map/jsgkf,rgkf->srjf/dot_general | solution.py:120
  94.5 0.0 copy-start.3
  94.6 1.6 %copy.28 = bf16[128,16,2,512]{0,3,2,1:T(8,128)(2,1)S(1)} copy(bf16[128,16,2,512]{0,1,2,3:T(8,128)(2,1)S(1)} %fusion) | data formatting | bytes 8388608 | tf_op jit(solution)/shard_map/convert_element_type | solution.py:145
  96.2 0.0 copy-done.3
  96.2 4.9 %divide_convert_fusion = bf16[128,16,1024]{2,0,1:T(8,128)(2,1)S(1)} fusion(f32[128,16]{0,1:T(8,128)S(1)} %convolution_maximum_fusion, bf16[128,16,1024]{0,2,1:T(8,128)(2,1)S(1)} %bitcast.33, bf16[1024,1024,1]{1,0,2:T(8,128)(2,1)S(1)} %copy-done.3), kind=kOutput, calls=%fused_computation.1 | convolution fusion | flops 4301258752 | bytes 10493952 | tf_op jit(solution)/shard_map/dot_general | solution.py:147
  101.1 4.3 %copy.30 = bf16[128,16,1024]{2,1,0:T(8,128)(2,1)} copy(bf16[128,16,1024]{2,0,1:T(8,128)(2,1)S(1)} %divide_convert_fusion) | data formatting | bytes 8388608 | tf_op jit(solution)/shard_map/convert_element_type | solution.py:152
  (1 shorter events, 0.0 us)
Async XLA Ops:
  6.5 66.8 %all-gather.2.cloned.1.call-start = ((), (), s32[]{:S(2)}) async-start(), calls=%async_computation | async-start | bytes 4456448 | tf_op jit(solution)/shard_map/all_gather | solution.py:129
  8.8 3.4 %copy-start = (bf16[4096,1024]{1,0:T(8,128)(2,1)S(1)}, bf16[4096,1024]{1,0:T(8,128)(2,1)}, u32[]{:S(2)}) copy-start(bf16[4096,1024]{1,0:T(8,128)(2,1)} %constant.21.clone.table_ref) | copy-start | bytes 25165828
  12.2 1.2 %copy-start.1 = (bf16[8,16,4096]{2,1,0:T(8,128)(2,1)S(1)}, bf16[8,16,4096]{2,1,0:T(8,128)(2,1)}, u32[]{:S(2)}) copy-start(bf16[8,16,4096]{2,1,0:T(8,128)(2,1)} %raw_ref.1) | copy-start | bytes 3145732
  13.4 10.8 %copy-start.2 = (s32[256]{0:T(256)S(1)}, s32[256]{0:T(256)}, u32[]{:S(2)}) copy-start(s32[256]{0:T(256)} %param.12) | copy-start | bytes 3076
  94.5 1.6 %copy-start.3 = (bf16[1024,1024,1]{1,0,2:T(8,128)(2,1)S(1)}, bf16[1024,1024,1]{1,0,2:T(8,128)(2,1)}, u32[]{:S(2)}) copy-start(bf16[1024,1024,1]{1,0,2:T(8,128)(2,1)} %constant.30) | copy-start | bytes 6291460
Sparse Core Ops, SparseCore 0:
  20.1 53.2 all-gather.1

commit v3 on v2

--- a/solution.py
+++ b/solution.py
@@ -1,3 +1,4 @@
+import functools
 import math
 
 import jax
@@ -114,19 +115,155 @@
     )(raw, band, taps, mask, jnp.asarray(dft_table()))
 
 
+PIECES = 2
+
+
+def gather_kernel(count, own_ref, out_ref, own_sem, up_sem, down_sem, y_sem, core_sem, recv_sem):
+    levels = count // 4
+    me = lax.axis_index("chan")
+    level, side, core = me // 4, (me // 2) % 2, me % 2
+    y_peer = me + 2 - 4 * side
+    core_peer = me + 1 - 2 * core
+    has_up, has_down = level < levels - 1, level > 0
+    barrier = pltpu.get_barrier_semaphore()
+
+    def greet(peer):
+        pl.semaphore_signal(barrier, inc=1, device_id={"chan": peer}, device_id_type=pl.DeviceIdType.MESH)
+
+    greet(y_peer)
+    greet(core_peer)
+
+    @pl.when(has_up)
+    def _():
+        greet(me + 4)
+
+    @pl.when(has_down)
+    def _():
+        greet(me - 4)
+
+    pl.semaphore_wait(barrier, 2 + has_up.astype(jnp.int32) + has_down.astype(jnp.int32))
+
+    height = own_ref.shape[0] // PIECES
+
+    def send(block, piece, sems, peer, source=None):
+        rows = pl.ds(piece * height, height)
+        place = out_ref.at[block, rows]
+        return pltpu.make_async_remote_copy(
+            src_ref=place if source is None else source.at[rows],
+            dst_ref=place,
+            send_sem=sems.at[block, piece],
+            recv_sem=recv_sem.at[block, piece],
+            device_id={"chan": peer},
+            device_id_type=pl.DeviceIdType.MESH,
+        )
+
+    def arrived(block, piece):
+        send(block, piece, y_sem, y_peer).wait_recv()
+
+    keep = pltpu.make_async_copy(own_ref, out_ref.at[me], own_sem)
+    keep.start()
+    for piece in range(PIECES):
+
+        @pl.when(has_up)
+        def _():
+            send(me, piece, up_sem, me + 4, own_ref).start()
+
+        @pl.when(has_down)
+        def _():
+            send(me, piece, down_sem, me - 4, own_ref).start()
+
+        send(me, piece, y_sem, y_peer, own_ref).start()
+        send(me, piece, core_sem, core_peer, own_ref).start()
+
+    def across(far):
+        for piece in range(PIECES):
+            block = far * 4 + (1 - side) * 2 + core
+            arrived(block, piece)
+            send(block, piece, core_sem, core_peer).start()
+
+    def each(distance, act):
+        for way in (1, -1):
+            far = level + way * distance
+            if distance == 0 and way == -1:
+                continue
+
+            @pl.when((far >= 0) & (far < levels))
+            def _():
+                act(far, way)
+
+    for distance in range(1, levels + 1):
+        if distance < levels:
+
+            def along(far, way):
+                block = far * 4 + side * 2 + core
+                for piece in range(PIECES):
+                    arrived(block, piece)
+                    if way == 1:
+
+                        @pl.when(has_down)
+                        def _():
+                            send(block, piece, down_sem, me - 4).start()
+                    else:
+
+                        @pl.when(has_up)
+                        def _():
+                            send(block, piece, up_sem, me + 4).start()
+
+                    send(block, piece, y_sem, y_peer).start()
+                    send(block, piece, core_sem, core_peer).start()
+
+            each(distance, along)
+        each(distance - 1, lambda far, way: across(far))
+
+    for far in range(levels):
+        for piece in range(PIECES):
+            mine, other = far * 4 + side * 2 + core, far * 4 + (1 - side) * 2 + core
+            arrived(far * 4 + side * 2 + 1 - core, piece)
+            arrived(far * 4 + (1 - side) * 2 + 1 - core, piece)
+            send(mine, piece, y_sem, y_peer).wait_send()
+            send(mine, piece, core_sem, core_peer).wait_send()
+            send(other, piece, core_sem, core_peer).wait_send()
+
+            @pl.when(has_up & (far <= level))
+            def _():
+                send(mine, piece, up_sem, me + 4).wait_send()
+
+            @pl.when(has_down & (far >= level))
+            def _():
+                send(mine, piece, down_sem, me - 4).wait_send()
+
+    keep.wait()
+
+
+def gather(own, count):
+    if count % 4 or count < 4:
+        return lax.all_gather(own, "chan", axis=0)
+    sems = pltpu.SemaphoreType.DMA((count, PIECES))
+    return pl.pallas_call(
+        lambda *refs: gather_kernel(count, *refs),
+        out_shape=jax.ShapeDtypeStruct((count,) + own.shape, own.dtype),
+        in_specs=[pl.BlockSpec(memory_space=pltpu.VMEM)],
+        out_specs=pl.BlockSpec(memory_space=pltpu.VMEM),
+        scratch_shapes=[pltpu.SemaphoreType.DMA, sems, sems, sems, sems, sems],
+        compiler_params=pltpu.CompilerParams(
+            collective_id=0, has_side_effects=True, vmem_limit_bytes=40 * 2**20
+        ),
+    )(own)
+
+
 def cross_stack(sources, receivers):
     turned = jnp.stack([-sources[:, :, 1], sources[:, :, 0]], axis=2)
     paired = jnp.stack([sources, turned], axis=0)
     return jnp.einsum("jsgkf,rgkf->srjf", paired, receivers, preferred_element_type=jnp.float32)
 
 
-def body(raw_strain, bandpass, whiten_taps, segment_mask, channel_block, source_block):
+def body(chan_count, raw_strain, bandpass, whiten_taps, segment_mask, channel_block, source_block):
     seg_count, chan_rows, sample_count = raw_strain.shape
     chan_start = lax.axis_index("chan") * chan_rows
     mask_all = segment_mask.astype(jnp.float32)
     mask_here = lax.dynamic_slice_in_dim(mask_all, chan_start, chan_rows, 1)
     spectra = front(raw_strain, bandpass, whiten_taps, mask_here)
-    gathered = lax.all_gather(spectra, "chan", axis=0, tiled=True).reshape(-1, seg_count, 2, FBINS)
+    gathered = gather(spectra, chan_count).reshape(-1, seg_count, 2, FBINS)
     spectra = spectra.reshape(chan_rows, seg_count, 2, FBINS)
     member = channel_block == source_block[0]
     order = jnp.arange(member.shape[0], dtype=jnp.int32)
@@ -162,4 +299,4 @@
         P("groups"),
     )
     out_specs = P(None, ("groups", "chan"), None)
-    return jax.shard_map(body, mesh=mesh, in_specs=in_specs, out_specs=out_specs, check_vma=False)
+    return jax.shard_map(functools.partial(body, mesh.shape["chan"]), mesh=mesh, in_specs=in_specs, out_specs=out_specs, check_vma=False)

time: 113 us -> 77 us (0.68)
  waiting for transfers between devices: 48.7 us -> 0 us
  Pallas kernels: 6.5 us -> 35.7 us
  between operations: 14.1 us -> 0.76 us
  matrix products: 15.7 us -> 13.8 us
  local copies, waits for them, and re-layouts: 22.3 us -> 20.7 us
    all_gather x1 -> x0, waiting for transfers between devices: 48.7 us -> none  [body(): lax.all_gather(spectra, 'chan', axis=0, tiled=True)]
    pallas_call x0 -> x1, Pallas kernels: none -> 30 us  [gather(): pl.pallas_call(lambda *refs: gather_kernel(count, *refs), out_shape=jax.S...]
    dot_general x1, matrix products: 7.08 us -> 4.89 us  [body(): jnp.einsum('sc,cgkf->sgkf', selector, gathered, preferred_element_type=jn...]
    reshape x1, local copies, waits for them, and re-layouts: 3.63 us -> 2.06 us  [body(): spectra = spectra.reshape(chan_rows, seg_count, 2, FBINS)]
    unnamed x8 -> x6, local copies, waits for them, and re-layouts: 4.61 us -> 4.61 us
  transfers between devices with their start and end apart: 1 -> 0, of which waited for: 1 -> 0; matrix products, arithmetic and copies ran while one was open for 4% -> 0% of each run, Pallas kernels for 0% -> 0%
where the time goes in v3:
time: 77 us; the launch traced here: 76.5 us
  Pallas kernels  35.7 us (46%)
  local copies, waits for them, and re-layouts  20.7 us (27%)
  matrix products  13.8 us (18%)
  other arithmetic  5.57 us (7%)
    pallas_call x1, Pallas kernels, gather(): pl.pallas_call(lambda *refs: gather_kernel(count, *refs), out_shape=jax.S...  30 us
    another operation x1, local copies, waits for them, and re-layouts, cross_stack(): paired = jnp.stack([sources, turned], axis=0)  7.87 us
    pallas_call x1, Pallas kernels, front(): pl.pallas_call(front_kernel, grid=(samples // depth,), out_shape=jax.Shap...  5.78 us
    dot_general x1, matrix products, body(): jnp.dot(stacked.reshape(BLOCK * chan_rows, 2 * FBINS), lag_table, preferr...  5.1 us
    dot_general x1, matrix products, body(): jnp.einsum('sc,cgkf->sgkf', selector, gathered, preferred_element_type=jn...  4.89 us
    unnamed x6, local copies, waits for them, and re-layouts  4.61 us
    convert_element_type x1, local copies, waits for them, and re-layouts, body(): (lagged * factor / jnp.maximum(counts, 1.0)[:, :, None]).astype(jnp.bfloa...  4.34 us
    dot_general x1, matrix products, cross_stack(): jnp.einsum('jsgkf,rgkf->srjf', paired, receivers, preferred_element_type=...  3.51 us

profile of v3, /device:TPU:0, one launch (start us, length us, event | category | flops | bytes accessed | tf_op | source)
XLA Modules:
  0.0 76.5 jit_solution(13351697845092497094)
XLA Ops:
  0.7 0.7 broadcast_compare_fusion
  1.3 0.7 pad_convert_fusion.1.band_ref
  2.0 0.1 convert_reduce_fusion
  2.1 0.7 convert_element_type.26
  2.8 0.1 dynamic-slice_bitcast_fusion
  2.9 0.3 convolution_maximum_fusion
  3.1 0.1 copy.23
  3.2 0.7 pad_convert_fusion.taps_ref
  3.9 0.1 reshape.23.mask_ref
  4.0 0.0 copy-start
  4.0 3.4 %copy-done = bf16[4096,1024]{1,0:T(8,128)(2,1)S(1)} copy-done((bf16[4096,1024]{1,0:T(8,128)(2,1)S(1)}, bf16[4096,1024]{1,0:T(8,128)(2,1)}, u32[]{:S(2)}) %copy-start) | copy-done | bytes 8388632
  7.4 0.0 copy-start.1
  7.4 1.2 %copy-done.1 = bf16[8,16,4096]{2,1,0:T(8,128)(2,1)S(1)} copy-done((bf16[8,16,4096]{2,1,0:T(8,128)(2,1)S(1)}, bf16[8,16,4096]{2,1,0:T(8,128)(2,1)}, u32[]{:S(2)}) %copy-start.1) | copy-done | bytes 1048600
  8.6 5.8 %shard_map.82.refs_0_ = bf16[128,1024]{1,0:T(8,128)(2,1)S(1)} custom-call(bf16[8,16,4096]{2,1,0:T(8,128)(2,1)S(1)} %copy-done.1, f32[1,128]{1,0:T(1,128)S(1)} %pad_convert_fusion.1.band_ref, f32[16,128]{1,0:T(8,128)S(1)} %pad_convert_fusion.taps_ref, f32[128,1]{1,0:T(8,128)S(1)} %reshape.23.mask_ref, bf16[4096,1024]{1,0:T(8,128)(2,1)S(1)} %copy-done), custom_call_target="tpu_custom_call" | custom-call | flops 2000000000 | bytes 10000000 | tf_op jit(solution)/shard_map/pallas_call | solution.py:95
  14.4 2.1 %copy.32 = bf16[16,8,2,512,1]{0,1,2,4,3:T(8,128)(2,1)S(1)} copy(bf16[16,8,2,512,1]{3,1,2,0,4:T(8,128)(2,1)S(1)} %bitcast.32) | data formatting | bytes 524288 | tf_op jit(solution)/shard_map/reshape | solution.py:267
  16.5 30.0 %shard_map.83 = bf16[16,128,1024]{2,1,0:T(8,128)(2,1)S(1)} custom-call(bf16[128,1024]{1,0:T(8,128)(2,1)S(1)} %shard_map.82.refs_0_), custom_call_target="tpu_custom_call" | custom-call | tf_op jit(solution)/shard_map/pallas_call | solution.py:242
  46.4 4.9 %fusion.3 = bf16[128,8,2,512]{3,0,2,1:T(8,128)(2,1)S(1)} fusion(bf16[256,8,2,512]{3,1,2,0:T(8,128)(2,1)S(1)} %bitcast.31, s32[256]{0:T(256)S(1)} %convert_reduce_fusion, pred[256]{0:T(512)(128)(4,1)S(1)} %broadcast_compare_fusion), kind=kOutput, calls=%fused_computation.7 | convolution fusion | flops 537985024 | bytes 6292736 | tf_op jit(solution)/shard_map/sc,cgkf->sgkf/dot_general | solution.py:276
  51.3 0.1 slice_negate_fusion
  51.5 0.2 maximum_bitcast_fusion
  51.7 2.4 %pad_maximum_fusion = bf16[2,128,8,2,512]{4,1,3,2,0:T(8,128)(2,1)} fusion(bf16[1,128,8,2,512]{4,1,3,2,0:T(8,128)(2,1)S(1)} %maximum_bitcast_fusion, bf16[1,128,8,2,512]{4,1,3,2,0:T(8,128)(2,1)S(1)} %bitcast.33), kind=kLoop, calls=%fused_computation.3 | loop fusion | flops 2097152 | bytes 8388608 | tf_op jit(solution)/shard_map/stack | solution.py:256
  54.1 7.9 %copy.27 = bf16[2,128,8,2,512]{1,2,3,0,4:T(8,128)(2,1)} copy(bf16[2,128,8,2,512]{4,1,3,2,0:T(8,128)(2,1)} %pad_maximum_fusion) | data formatting | bytes 8388608 | tf_op jit(solution)/shard_map/stack | solution.py:256
  61.9 3.5 %fusion = bf16[128,16,2,512]{0,1,2,3:T(8,128)(2,1)S(1)} fusion(bf16[16,8,2,512,1]{0,1,2,4,3:T(8,128)(2,1)S(1)} %copy.32, bf16[2,128,8,2,512]{1,2,3,0,4:T(8,128)(2,1)} %copy.27), kind=kOutput, calls=%fused_computation.2 | convolution fusion | flops 69206016 | bytes 8650752 | tf_op jit(solution)/shard_map/jsgkf,rgkf->srjf/dot_general | solution.py:257
  65.5 0.0 copy-start.2
  65.5 1.6 %copy.28 = bf16[128,16,2,512]{0,3,2,1:T(8,128)(2,1)S(1)} copy(bf16[128,16,2,512]{0,1,2,3:T(8,128)(2,1)S(1)} %fusion) | data formatting | bytes 8388608 | tf_op jit(solution)/shard_map/convert_element_type | solution.py:282
  67.1 0.0 copy-done.2
  67.1 5.1 %divide_convert_fusion = bf16[128,16,1024]{2,0,1:T(8,128)(2,1)S(1)} fusion(f32[128,16]{0,1:T(8,128)S(1)} %convolution_maximum_fusion, bf16[128,16,1024]{0,2,1:T(8,128)(2,1)S(1)} %bitcast.34, bf16[1024,1024,1]{1,0,2:T(8,128)(2,1)S(1)} %copy-done.2), kind=kOutput, calls=%fused_computation.1 | convolution fusion | flops 4301258752 | bytes 10493952 | tf_op jit(solution)/shard_map/dot_general | solution.py:284
  72.2 4.3 %copy.30 = bf16[128,16,1024]{2,1,0:T(8,128)(2,1)} copy(bf16[128,16,1024]{2,0,1:T(8,128)(2,1)S(1)} %divide_convert_fusion) | data formatting | bytes 8388608 | tf_op jit(solution)/shard_map/convert_element_type | solution.py:289
Async XLA Ops:
  4.0 3.4 %copy-start = (bf16[4096,1024]{1,0:T(8,128)(2,1)S(1)}, bf16[4096,1024]{1,0:T(8,128)(2,1)}, u32[]{:S(2)}) copy-start(bf16[4096,1024]{1,0:T(8,128)(2,1)} %constant.21.clone.table_ref) | copy-start | bytes 25165828
  7.4 1.2 %copy-start.1 = (bf16[8,16,4096]{2,1,0:T(8,128)(2,1)S(1)}, bf16[8,16,4096]{2,1,0:T(8,128)(2,1)}, u32[]{:S(2)}) copy-start(bf16[8,16,4096]{2,1,0:T(8,128)(2,1)} %raw_ref.1) | copy-start | bytes 3145732
  65.5 1.6 %copy-start.2 = (bf16[1024,1024,1]{1,0,2:T(8,128)(2,1)S(1)}, bf16[1024,1024,1]{1,0,2:T(8,128)(2,1)}, u32[]{:S(2)}) copy-start(bf16[1024,1024,1]{1,0,2:T(8,128)(2,1)} %constant.30) | copy-start | bytes 6291460

commit v4 on v3

--- a/solution.py
+++ b/solution.py
@@ -251,10 +251,71 @@
     )(own)
 
 
-def cross_stack(sources, receivers):
-    turned = jnp.stack([-sources[:, :, 1], sources[:, :, 0]], axis=2)
-    paired = jnp.stack([sources, turned], axis=0)
-    return jnp.einsum("jsgkf,rgkf->srjf", paired, receivers, preferred_element_type=jnp.float32)
+SOURCES_STEP = 16
+
+
+def back_kernel(index_ref, all_ref, own_ref, scale_ref, lag_ref, out_ref, local, first, stacked):
+    rows, segs = local.shape[1], local.shape[0]
+    step = pl.program_id(0)
+
+    @pl.when(step == 0)
+    def _():
+        for r in range(0, rows, 2):
+            pair = own_ref[r * segs : (r + 2) * segs].astype(jnp.float32)
+            for k in range(2):
+                for g in range(segs):
+                    local[g, r + k : r + k + 1, :] = pair[k * segs + g : k * segs + g + 1]
+
+    for s in range(SOURCES_STEP):
+        channel = index_ref[step * SOURCES_STEP + s]
+        pair = all_ref[pl.ds(pl.multiple_of((channel // 2) * 2 * segs, 2 * segs), 2 * segs), :]
+        pair = pair.astype(jnp.float32)
+        first[s] = jnp.where(channel % 2 == 0, pair[:segs], pair[segs:])
+
+    for j in range(FBINS // 128):
+        re, im = slice(j * 128, (j + 1) * 128), slice(FBINS + j * 128, FBINS + (j + 1) * 128)
+        far = [(local[g, :, re], local[g, :, im]) for g in range(segs)]
+        for s in range(SOURCES_STEP):
+            total_re, total_im = 0.0, 0.0
+            for g in range(segs):
+                a = jnp.broadcast_to(first[s, g : g + 1, re], (rows, 128))
+                b = jnp.broadcast_to(first[s, g : g + 1, im], (rows, 128))
+                total_re = total_re + a * far[g][0] + b * far[g][1]
+                total_im = total_im + a * far[g][1] - b * far[g][0]
+            stacked[s * rows : (s + 1) * rows, re] = total_re.astype(jnp.bfloat16)
+            stacked[s * rows : (s + 1) * rows, im] = total_im.astype(jnp.bfloat16)
+
+    lagged = jnp.dot(stacked[...], lag_ref[...], preferred_element_type=jnp.float32) * scale_ref[...]
+    out_ref[...] = lagged.astype(jnp.bfloat16).reshape(SOURCES_STEP, rows, LAGS)
+
+
+def back(index, gathered, own, scale, rows, segs):
+    width = 2 * FBINS
+    once = lambda *shape: pl.BlockSpec(
+        shape, lambda i, *_: (0,) * len(shape), pipeline_mode=pl.Buffered(1)
+    )
+    return pl.pallas_call(
+        back_kernel,
+        out_shape=jax.ShapeDtypeStruct((BLOCK, rows, LAGS), jnp.bfloat16),
+        grid_spec=pltpu.PrefetchScalarGridSpec(
+            num_scalar_prefetch=1,
+            grid=(BLOCK // SOURCES_STEP,),
+            in_specs=[
+                once(*gathered.shape),
+                once(*own.shape),
+                pl.BlockSpec((SOURCES_STEP * rows, 1), lambda i, *_: (i, 0)),
+                once(width, LAGS),
+            ],
+            out_specs=pl.BlockSpec((SOURCES_STEP, rows, LAGS), lambda i, *_: (i, 0, 0)),
+            scratch_shapes=[
+                pltpu.VMEM((segs, rows, width), jnp.float32),
+                pltpu.VMEM((SOURCES_STEP, segs, width), jnp.float32),
+                pltpu.VMEM((SOURCES_STEP * rows, width), jnp.bfloat16),
+            ],
+        ),
+        compiler_params=pltpu.CompilerParams(vmem_limit_bytes=44 * 2**20),
+        cost_estimate=pl.CostEstimate(flops=5 * 10**9, bytes_accessed=10**7, transcendentals=0),
+    )(index, gathered, own, scale, jnp.asarray(lag_table_np()))
 
 
 def body(chan_count, raw_strain, bandpass, whiten_taps, segment_mask, channel_block, source_block):
@@ -263,30 +324,18 @@
     mask_all = segment_mask.astype(jnp.float32)
     mask_here = lax.dynamic_slice_in_dim(mask_all, chan_start, chan_rows, 1)
     spectra = front(raw_strain, bandpass, whiten_taps, mask_here)
-    gathered = gather(spectra, chan_count).reshape(-1, seg_count, 2, FBINS)
-    spectra = spectra.reshape(chan_rows, seg_count, 2, FBINS)
+    gathered = gather(spectra, chan_count).reshape(-1, 2 * FBINS)
     member = channel_block == source_block[0]
     order = jnp.arange(member.shape[0], dtype=jnp.int32)
     below = member[None, :] & (order[None, :] < order[:, None])
     member_rank = jnp.sum(below.astype(jnp.int32), axis=1)
     chosen = member[None, :] & (member_rank[None, :] == jnp.arange(BLOCK, dtype=jnp.int32)[:, None])
-    selector = chosen.astype(jnp.bfloat16)
+    index = jnp.sum(jnp.where(chosen, order[None, :], 0), axis=1)
     source_mask = jnp.dot(mask_all, chosen.astype(jnp.float32).T)
     counts = jnp.dot(source_mask.T, mask_here)
-    sources = jnp.einsum(
-        "sc,cgkf->sgkf",
-        selector,
-        gathered,
-        preferred_element_type=jnp.float32,
-    ).astype(jnp.bfloat16)
-    stacked = cross_stack(sources, spectra).astype(jnp.bfloat16)
-    lag_table = jnp.asarray(lag_table_np())
-    lagged = jnp.dot(
-        stacked.reshape(BLOCK * chan_rows, 2 * FBINS), lag_table, preferred_element_type=jnp.float32
-    )
-    lagged = lagged.reshape(BLOCK, chan_rows, LAGS)
     factor = 2.0 / (SAMPLES * math.sqrt(FBINS))
-    return (lagged * factor / jnp.maximum(counts, 1.0)[:, :, None]).astype(jnp.bfloat16)
+    scale = (factor / jnp.maximum(counts, 1.0)).reshape(BLOCK * chan_rows, 1)
+    return back(index, gathered, spectra, scale, chan_rows, seg_count)
 
 
 def solution(mesh):

time: 77 us -> 66.2 us (0.86)
  Pallas kernels: 35.7 us -> 56.4 us
  local copies, waits for them, and re-layouts: 20.7 us -> 5.49 us
  matrix products: 13.8 us -> 0.26 us
  other arithmetic: 5.57 us -> 2.98 us
    pallas_call x0 -> x1, Pallas kernels: none -> 20.6 us  [back(): pl.pallas_call(back_kernel, out_shape=jax.ShapeDtypeStruct((BLOCK, rows,...]
    dot_general x3 -> x0, matrix products: 13.5 us -> none  [the longest x1 5.1 us: body(): jnp.dot(stacked.reshape(BLOCK * chan_rows, 2 * FBINS), lag_table, preferr...]
    another operation x1 -> x0, local copies, waits for them, and re-layouts: 7.87 us -> none  [cross_stack(): paired = jnp.stack([sources, turned], axis=0)]
    convert_element_type x2 -> x0, local copies, waits for them, and re-layouts: 5.96 us -> none  [the longest x1 4.34 us: body(): (lagged * factor / jnp.maximum(counts, 1.0)[:, :, None]).astype(jnp.bfloa...]
    another operation x2 -> x0, other arithmetic: 2.57 us -> none  [cross_stack(): paired = jnp.stack([sources, turned], axis=0)]
    reshape x1, local copies, waits for them, and re-layouts: 2.06 us -> 0.57 us  [body(): scale = (factor / jnp.maximum(counts, 1.0)).reshape(BLOCK * chan_rows, 1)]
where the time goes in v4:
time: 66.2 us; the launch traced here: 65.9 us
  Pallas kernels  56.4 us (85%)
  local copies, waits for them, and re-layouts  5.49 us (8%)
  other arithmetic  2.98 us (5%)
  between operations  0.72 us (1%)
    pallas_call x1, Pallas kernels, gather(): pl.pallas_call(lambda *refs: gather_kernel(count, *refs), out_shape=jax.S...  30 us
    pallas_call x1, Pallas kernels, back(): pl.pallas_call(back_kernel, out_shape=jax.ShapeDtypeStruct((BLOCK, rows,...  20.6 us
    pallas_call x1, Pallas kernels, front(): pl.pallas_call(front_kernel, grid=(samples // depth,), out_shape=jax.Shap...  5.78 us
    unnamed x6, local copies, waits for them, and re-layouts  4.61 us

profile of v4, /device:TPU:0, one launch (start us, length us, event | category | flops | bytes accessed | tf_op | source)
XLA Modules:
  0.0 65.9 jit_solution(1286290022612525558)
XLA Ops:
  0.7 0.7 %broadcast_compare_fusion = pred[256]{0:T(512)(128)(4,1)S(1)} fusion(s32[256]{0:T(256)} %param.12, s32[]{:T(128)} %bitcast.6), kind=kLoop, calls=%fused_computation.15 | loop fusion | flops 256 | bytes 1284 | tf_op jit(solution)/shard_map/eq | solution.py:328
  1.3 0.7 %pad_convert_fusion.1.band_ref = f32[1,128]{1,0:T(1,128)S(1)} fusion(bf16[1,64]{1,0:T(2,128)(2,1)} %bitcast.8), kind=kLoop, calls=%fused_computation.14 | loop fusion | flops 128 | bytes 640 | tf_op jit(solution)/shard_map/jit(_pad)/pad | solution.py:90
  2.0 0.1 convert_reduce_fusion
  2.1 0.1 select_reduce_fusion.index_ref
  2.2 0.7 %convert_element_type.14 = f32[8,256]{1,0:T(8,128)S(1)} convert(s32[8,256]{1,0:T(8,128)} %param.11) | non-fusion elementwise | flops 2048 | bytes 16384 | tf_op jit(solution)/shard_map/convert_element_type | solution.py:324
  2.9 0.1 dynamic-slice_bitcast_fusion
  3.0 0.3 fusion
  3.3 0.1 copy.16
  3.3 0.7 %pad_convert_fusion.taps_ref = f32[16,128]{1,0:T(8,128)S(1)} fusion(bf16[16,64]{1,0:T(8,128)(2,1)} %param.10), kind=kLoop, calls=%fused_computation.11 | loop fusion | flops 2048 | bytes 10240 | tf_op jit(solution)/shard_map/jit(_pad)/pad | solution.py:91
  4.1 0.1 reshape.14.mask_ref
  4.1 0.1 copy.18
  4.2 0.0 copy-start
  4.2 3.4 %copy-done = bf16[4096,1024]{1,0:T(8,128)(2,1)S(1)} copy-done((bf16[4096,1024]{1,0:T(8,128)(2,1)S(1)}, bf16[4096,1024]{1,0:T(8,128)(2,1)}, u32[]{:S(2)}) %copy-start) | copy-done | bytes 8388632
  7.6 0.0 copy-start.1
  7.6 1.2 %copy-done.1 = bf16[8,16,4096]{2,1,0:T(8,128)(2,1)S(1)} copy-done((bf16[8,16,4096]{2,1,0:T(8,128)(2,1)S(1)}, bf16[8,16,4096]{2,1,0:T(8,128)(2,1)}, u32[]{:S(2)}) %copy-start.1) | copy-done | bytes 1048600
  8.8 5.8 %shard_map.82.refs_0_.own_ref = bf16[128,1024]{1,0:T(8,128)(2,1)S(1)} custom-call(bf16[8,16,4096]{2,1,0:T(8,128)(2,1)S(1)} %copy-done.1, f32[1,128]{1,0:T(1,128)S(1)} %pad_convert_fusion.1.band_ref, f32[16,128]{1,0:T(8,128)S(1)} %pad_convert_fusion.taps_ref, f32[128,1]{1,0:T(8,128)S(1)} %reshape.14.mask_ref, bf16[4096,1024]{1,0:T(8,128)(2,1)S(1)} %copy-done), custom_call_target="tpu_custom_call" | custom-call | flops 2000000000 | bytes 10000000 | tf_op jit(solution)/shard_map/pallas_call | solution.py:95
  14.6 0.0 copy-start.2
  14.6 0.6 reshape.15.scale_ref
  15.2 30.0 %shard_map.83 = bf16[16,128,1024]{2,1,0:T(8,128)(2,1)S(1)} custom-call(bf16[128,1024]{1,0:T(8,128)(2,1)S(1)} %shard_map.82.refs_0_.own_ref), custom_call_target="tpu_custom_call" | custom-call | tf_op jit(solution)/shard_map/pallas_call | solution.py:242
  45.2 0.0 copy-done.2
  45.2 20.6 %shard_map.84 = bf16[128,16,1024]{2,1,0:T(8,128)(2,1)} custom-call(s32[128]{0:T(128)S(1)} %select_reduce_fusion.index_ref, bf16[2048,1024]{1,0:T(8,128)(2,1)S(1)} %bitcast.7, bf16[128,1024]{1,0:T(8,128)(2,1)S(1)} %shard_map.82.refs_0_.own_ref, f32[2048,1]{1,0:T(8,128)S(1)} %reshape.15.scale_ref, bf16[1024,1024]{1,0:T(8,128)(2,1)S(1)} %copy-done.2), custom_call_target="tpu_custom_call" | custom-call | flops 5000000000 | bytes 10000000 | tf_op jit(solution)/shard_map/pallas_call | solution.py:297
Async XLA Ops:
  4.2 3.4 %copy-start = (bf16[4096,1024]{1,0:T(8,128)(2,1)S(1)}, bf16[4096,1024]{1,0:T(8,128)(2,1)}, u32[]{:S(2)}) copy-start(bf16[4096,1024]{1,0:T(8,128)(2,1)} %constant.21.clone.table_ref) | copy-start | bytes 25165828
  7.6 1.2 %copy-start.1 = (bf16[8,16,4096]{2,1,0:T(8,128)(2,1)S(1)}, bf16[8,16,4096]{2,1,0:T(8,128)(2,1)}, u32[]{:S(2)}) copy-start(bf16[8,16,4096]{2,1,0:T(8,128)(2,1)} %raw_ref.1) | copy-start | bytes 3145732
  14.6 30.6 %copy-start.2 = (bf16[1024,1024]{1,0:T(8,128)(2,1)S(1)}, bf16[1024,1024]{1,0:T(8,128)(2,1)}, u32[]{:S(2)}) copy-start(bf16[1024,1024]{1,0:T(8,128)(2,1)} %constant.22.clone.lag_ref) | copy-start | bytes 6291460

commit v5 on v4

--- a/solution.py
+++ b/solution.py
@@ -48,7 +48,9 @@
 
     @pl.when(step == 0)
     def _():
-        matrix = toeplitz(band_ref[...])
+        widen = lambda x: jnp.pad(x.astype(jnp.float32), ((0, 0), (0, 128 - x.shape[1])))
+        matrix = toeplitz(widen(band_ref[...]))
+        taps = widen(taps_ref[...])
         power = jnp.zeros((segs * rows, 128), jnp.float32)
         for b in range(blocks):
             if b == 0:
@@ -62,7 +64,7 @@
         scale = 1.0 / jnp.sqrt(energy + 1e-05)
         inv[...] = jnp.broadcast_to(scale, (segs * rows, 128)).reshape(segs, rows, 128)
         for c in range(rows):
-            matrix = toeplitz(taps_ref[c : c + 1, :])
+            matrix = toeplitz(taps[c : c + 1, :])
             scale = inv[:, c, :]
             here = jnp.concatenate(
                 [filt[:, c, b * 128 : (b + 1) * 128] * scale for b in range(blocks)], axis=0
@@ -86,9 +88,7 @@
 
 def front(raw, bandpass, whiten_taps, mask_here):
     segs, rows, samples = raw.shape
-    pad = ((0, 0), (0, 128 - bandpass.shape[-1]))
-    band = jnp.pad(bandpass.astype(jnp.float32)[None], pad)
-    taps = jnp.pad(whiten_taps.astype(jnp.float32), pad)
+    band, taps = bandpass[None], whiten_taps
     mask = mask_here.T.reshape(rows * segs, 1)
     depth = 512
     whole = lambda *shape: pl.BlockSpec(shape, lambda i: (0,) * len(shape))
@@ -98,8 +98,8 @@
         out_shape=jax.ShapeDtypeStruct((rows * segs, 2 * FBINS), jnp.bfloat16),
         in_specs=[
             whole(segs, rows, samples),
-            whole(1, 128),
-            whole(rows, 128),
+            whole(*band.shape),
+            whole(*taps.shape),
             whole(rows * segs, 1),
             pl.BlockSpec((depth, 2 * FBINS), lambda i: (i, 0)),
         ],
@@ -110,12 +110,12 @@
             pltpu.VMEM((rows * segs, samples), jnp.float32),
             pltpu.VMEM((rows * segs, 2 * FBINS), jnp.float32),
         ],
-        compiler_params=pltpu.CompilerParams(vmem_limit_bytes=40 * 2**20),
+        compiler_params=pltpu.CompilerParams(vmem_limit_bytes=56 * 2**20),
         cost_estimate=pl.CostEstimate(flops=2 * 10**9, bytes_accessed=10**7, transcendentals=0),
     )(raw, band, taps, mask, jnp.asarray(dft_table()))
 
 
-PIECES = 2
+PIECES = 4
 
 
 def gather_kernel(count, own_ref, out_ref, own_sem, up_sem, down_sem, y_sem, core_sem, recv_sem):
@@ -175,45 +175,36 @@
         send(me, piece, y_sem, y_peer, own_ref).start()
         send(me, piece, core_sem, core_peer, own_ref).start()
 
-    def across(far):
-        for piece in range(PIECES):
-            block = far * 4 + (1 - side) * 2 + core
-            arrived(block, piece)
-            send(block, piece, core_sem, core_peer).start()
-
-    def each(distance, act):
-        for way in (1, -1):
+    def across(far, way, piece):
+        block = far * 4 + (1 - side) * 2 + core
+        arrived(block, piece)
+        send(block, piece, core_sem, core_peer).start()
+
+    def along(far, way, piece):
+        block = far * 4 + side * 2 + core
+        arrived(block, piece)
+
+        @pl.when(has_down if way == 1 else has_up)
+        def _():
+            sems, peer = (down_sem, me - 4) if way == 1 else (up_sem, me + 4)
+            send(block, piece, sems, peer).start()
+
+        send(block, piece, y_sem, y_peer).start()
+        send(block, piece, core_sem, core_peer).start()
+
+    def each(distance, piece, act):
+        for way in (1, -1) if distance else (1,):
             far = level + way * distance
-            if distance == 0 and way == -1:
-                continue
 
             @pl.when((far >= 0) & (far < levels))
             def _():
-                act(far, way)
+                act(far, way, piece)
 
     for distance in range(1, levels + 1):
-        if distance < levels:
-
-            def along(far, way):
-                block = far * 4 + side * 2 + core
-                for piece in range(PIECES):
-                    arrived(block, piece)
-                    if way == 1:
-
-                        @pl.when(has_down)
-                        def _():
-                            send(block, piece, down_sem, me - 4).start()
-                    else:
-
-                        @pl.when(has_up)
-                        def _():
-                            send(block, piece, up_sem, me + 4).start()
-
-                    send(block, piece, y_sem, y_peer).start()
-                    send(block, piece, core_sem, core_peer).start()
-
-            each(distance, along)
-        each(distance - 1, lambda far, way: across(far))
+        for piece in range(PIECES):
+            if distance < levels:
+                each(distance, piece, along)
+            each(distance - 1, piece, across)
 
     for far in range(levels):
         for piece in range(PIECES):
@@ -251,10 +242,11 @@
     )(own)
 
 
-SOURCES_STEP = 16
-
-
-def back_kernel(index_ref, all_ref, own_ref, scale_ref, lag_ref, out_ref, local, first, stacked):
+CHUNK = 16
+SOURCES_STEP = 2 * CHUNK
+
+
+def back_kernel(index_ref, all_ref, own_ref, scale_ref, lag_ref, out_ref, local, first, stacked_a, stacked_b):
     rows, segs = local.shape[1], local.shape[0]
     step = pl.program_id(0)
 
@@ -266,27 +258,28 @@
                 for g in range(segs):
                     local[g, r + k : r + k + 1, :] = pair[k * segs + g : k * segs + g + 1]
 
-    for s in range(SOURCES_STEP):
-        channel = index_ref[step * SOURCES_STEP + s]
-        pair = all_ref[pl.ds(pl.multiple_of((channel // 2) * 2 * segs, 2 * segs), 2 * segs), :]
-        pair = pair.astype(jnp.float32)
-        first[s] = jnp.where(channel % 2 == 0, pair[:segs], pair[segs:])
-
-    for j in range(FBINS // 128):
-        re, im = slice(j * 128, (j + 1) * 128), slice(FBINS + j * 128, FBINS + (j + 1) * 128)
-        far = [(local[g, :, re], local[g, :, im]) for g in range(segs)]
-        for s in range(SOURCES_STEP):
-            total_re, total_im = 0.0, 0.0
-            for g in range(segs):
-                a = jnp.broadcast_to(first[s, g : g + 1, re], (rows, 128))
-                b = jnp.broadcast_to(first[s, g : g + 1, im], (rows, 128))
-                total_re = total_re + a * far[g][0] + b * far[g][1]
-                total_im = total_im + a * far[g][1] - b * far[g][0]
-            stacked[s * rows : (s + 1) * rows, re] = total_re.astype(jnp.bfloat16)
-            stacked[s * rows : (s + 1) * rows, im] = total_im.astype(jnp.bfloat16)
-
-    lagged = jnp.dot(stacked[...], lag_ref[...], preferred_element_type=jnp.float32) * scale_ref[...]
-    out_ref[...] = lagged.astype(jnp.bfloat16).reshape(SOURCES_STEP, rows, LAGS)
+    for chunk, stacked in enumerate((stacked_a, stacked_b)):
+        base = chunk * CHUNK
+        for s in range(CHUNK):
+            channel = index_ref[step * SOURCES_STEP + base + s]
+            pair = all_ref[pl.ds(pl.multiple_of((channel // 2) * 2 * segs, 2 * segs), 2 * segs), :]
+            pair = pair.astype(jnp.float32)
+            first[base + s] = jnp.where(channel % 2 == 0, pair[:segs], pair[segs:])
+        for j in range(FBINS // 128):
+            re, im = slice(j * 128, (j + 1) * 128), slice(FBINS + j * 128, FBINS + (j + 1) * 128)
+            far = [(local[g, :, re], local[g, :, im]) for g in range(segs)]
+            for s in range(CHUNK):
+                total_re, total_im = 0.0, 0.0
+                for g in range(segs):
+                    a = jnp.broadcast_to(first[base + s, g : g + 1, re], (rows, 128))
+                    b = jnp.broadcast_to(first[base + s, g : g + 1, im], (rows, 128))
+                    total_re = total_re + a * far[g][0] + b * far[g][1]
+                    total_im = total_im + a * far[g][1] - b * far[g][0]
+                stacked[s * rows : (s + 1) * rows, re] = total_re.astype(jnp.bfloat16)
+                stacked[s * rows : (s + 1) * rows, im] = total_im.astype(jnp.bfloat16)
+        lagged = jnp.dot(stacked[...], lag_ref[...], preferred_element_type=jnp.float32)
+        lagged = lagged * scale_ref[base * rows : (base + CHUNK) * rows]
+        out_ref[base : base + CHUNK] = lagged.astype(jnp.bfloat16).reshape(CHUNK, rows, LAGS)
 
 
 def back(index, gathered, own, scale, rows, segs):
@@ -310,7 +303,8 @@
             scratch_shapes=[
                 pltpu.VMEM((segs, rows, width), jnp.float32),
                 pltpu.VMEM((SOURCES_STEP, segs, width), jnp.float32),
-                pltpu.VMEM((SOURCES_STEP * rows, width), jnp.bfloat16),
+                pltpu.VMEM((CHUNK * rows, width), jnp.bfloat16),
+                pltpu.VMEM((CHUNK * rows, width), jnp.bfloat16),
             ],
         ),
         compiler_params=pltpu.CompilerParams(vmem_limit_bytes=44 * 2**20),

time: 66.2 us -> 67.5 us (1.020)
  Pallas kernels: 56.4 us -> 62.2 us
  local copies, waits for them, and re-layouts: 5.49 us -> 2.48 us
  other arithmetic: 2.98 us -> 1.62 us
    pallas_call x1, Pallas kernels: 5.78 us -> 11 us  [front(): pl.pallas_call(front_kernel, grid=(samples // depth,), out_shape=jax.Shap...]
    unnamed x6, local copies, waits for them, and re-layouts: 4.61 us -> 0.96 us
    pad x2 -> x0, other arithmetic: 1.36 us -> none  [the longest x1 0.71 us: front(): taps = jnp.pad(whiten_taps.astype(jnp.float32), pad)]
    pallas_call x1, Pallas kernels: 30 us -> 31.2 us  [gather(): pl.pallas_call(lambda *refs: gather_kernel(count, *refs), out_shape=jax.S...]
    pallas_call x1, Pallas kernels: 20.6 us -> 19.9 us  [back(): pl.pallas_call(back_kernel, out_shape=jax.ShapeDtypeStruct((BLOCK, rows,...]
where the time goes in v5:
time: 67.5 us; the launch traced here: 67.2 us
  Pallas kernels  62.2 us (92%)
  local copies, waits for them, and re-layouts  2.48 us (4%)
  other arithmetic  1.62 us (2%)
  between operations  0.7 us (1%)
    pallas_call x1, Pallas kernels, gather(): pl.pallas_call(lambda *refs: gather_kernel(count, *refs), out_shape=jax.S...  31.2 us
    pallas_call x1, Pallas kernels, back(): pl.pallas_call(back_kernel, out_shape=jax.ShapeDtypeStruct((BLOCK, rows,...  19.9 us
    pallas_call x1, Pallas kernels, front(): pl.pallas_call(front_kernel, grid=(samples // depth,), out_shape=jax.Shap...  11 us

profile of v5, /device:TPU:0, one launch (start us, length us, event | category | flops | bytes accessed | tf_op | source)
XLA Modules:
  0.0 67.2 jit_solution(13304438045711980769)
XLA Ops:
  0.7 0.7 %broadcast_compare_fusion = pred[256]{0:T(512)(128)(4,1)S(1)} fusion(s32[256]{0:T(256)} %param.12, s32[]{:T(128)} %bitcast.6), kind=kLoop, calls=%fused_computation.13 | loop fusion | flops 256 | bytes 1284 | tf_op jit(solution)/shard_map/eq | solution.py:322
  1.3 0.1 convert_reduce_fusion
  1.5 0.1 select_reduce_fusion.index_ref
  1.6 0.7 %convert_element_type.8 = f32[8,256]{1,0:T(8,128)S(1)} convert(s32[8,256]{1,0:T(8,128)} %param.11) | non-fusion elementwise | flops 2048 | bytes 16384 | tf_op jit(solution)/shard_map/convert_element_type | solution.py:318
  2.3 0.1 dynamic-slice_bitcast_fusion
  2.4 0.3 fusion
  2.6 0.1 copy.16
  2.7 0.7 %reshape.14.mask_ref = f32[128,1]{1,0:T(8,128)} reshape(f32[16,8]{1,0:T(8,128)S(1)} %copy.16) | data formatting | bytes 1024 | tf_op jit(solution)/shard_map/reshape | solution.py:92
  3.4 0.1 copy.18
  3.5 11.0 %shard_map.82.refs_0_.own_ref = bf16[128,1024]{1,0:T(8,128)(2,1)} custom-call(bf16[8,16,4096]{2,1,0:T(8,128)(2,1)} %raw_ref.1, bf16[1,64]{1,0:T(2,128)(2,1)} %bitcast.8, bf16[16,64]{1,0:T(8,128)(2,1)} %taps_ref.1, f32[128,1]{1,0:T(8,128)} %reshape.14.mask_ref, bf16[4096,1024]{1,0:T(8,128)(2,1)} %constant.18.clone.table_ref), custom_call_target="tpu_custom_call" | custom-call | flops 2000000000 | bytes 10000000 | tf_op jit(solution)/shard_map/pallas_call | solution.py:95
  14.5 0.0 copy-start.1
  14.6 0.6 reshape.15.scale_ref
  15.1 0.0 copy-start
  15.1 0.9 %copy-done = bf16[128,1024]{1,0:T(8,128)(2,1)S(1)} copy-done((bf16[128,1024]{1,0:T(8,128)(2,1)S(1)}, bf16[128,1024]{1,0:T(8,128)(2,1)}, u32[]{:S(2)}) %copy-start) | copy-done | bytes 262168
  16.1 0.0 copy-start.2
  16.1 31.2 %shard_map.83 = bf16[16,128,1024]{2,1,0:T(8,128)(2,1)S(1)} custom-call(bf16[128,1024]{1,0:T(8,128)(2,1)S(1)} %copy-done), custom_call_target="tpu_custom_call" | custom-call | tf_op jit(solution)/shard_map/pallas_call | solution.py:233
  47.3 0.0 copy-done.1
  47.3 0.0 copy-done.2
  47.3 19.9 %shard_map.84 = bf16[128,16,1024]{2,1,0:T(8,128)(2,1)} custom-call(s32[128]{0:T(128)S(1)} %select_reduce_fusion.index_ref, bf16[2048,1024]{1,0:T(8,128)(2,1)S(1)} %bitcast.7, bf16[128,1024]{1,0:T(8,128)(2,1)S(1)} %copy-done.1, f32[2048,1]{1,0:T(8,128)S(1)} %reshape.15.scale_ref, bf16[1024,1024]{1,0:T(8,128)(2,1)S(1)} %copy-done.2), custom_call_target="tpu_custom_call" | custom-call | flops 5000000000 | bytes 10000000 | tf_op jit(solution)/shard_map/pallas_call | solution.py:290
Async XLA Ops:
  14.5 32.8 %copy-start.1 = (bf16[128,1024]{1,0:T(8,128)(2,1)S(1)}, bf16[128,1024]{1,0:T(8,128)(2,1)}, u32[]{:S(2)}) copy-start(bf16[128,1024]{1,0:T(8,128)(2,1)} %shard_map.82.refs_0_.own_ref) | copy-start | bytes 786436
  15.1 1.0 %copy-start = (bf16[128,1024]{1,0:T(8,128)(2,1)S(1)}, bf16[128,1024]{1,0:T(8,128)(2,1)}, u32[]{:S(2)}) copy-start(bf16[128,1024]{1,0:T(8,128)(2,1)} %shard_map.82.refs_0_.own_ref) | copy-start | bytes 786436
  16.1 31.2 %copy-start.2 = (bf16[1024,1024]{1,0:T(8,128)(2,1)S(1)}, bf16[1024,1024]{1,0:T(8,128)(2,1)}, u32[]{:S(2)}) copy-start(bf16[1024,1024]{1,0:T(8,128)(2,1)} %constant.19.clone.lag_ref) | copy-start | bytes 6291460

commit v6 on v5

--- a/solution.py
+++ b/solution.py
@@ -21,14 +21,19 @@
     return np.cos(angles).astype(jnp.bfloat16), (-np.sin(angles)).astype(jnp.bfloat16)
 
 
+def bin_order():
+    bins = KLO + np.arange(FBINS)
+    return np.concatenate([bins[bins % 2 == 0], bins[bins % 2 == 1]])
+
+
 def dft_table():
-    bins = KLO + np.arange(FBINS)
-    return np.concatenate(table(np.arange(SAMPLES)[:, None] * bins[None, :] % SAMPLES), axis=1)
+    even, odd = np.split(bin_order(), 2)
+    time = np.arange(SAMPLES // 2)[:, None]
+    return np.concatenate(table(time * even % SAMPLES) + table(time * odd % SAMPLES), axis=1)
 
 
 def lag_table_np():
-    bins = KLO + np.arange(FBINS)
-    return np.concatenate(table(bins[:, None] * (np.arange(LAGS) - LAGS // 2)[None, :] % SAMPLES), axis=0)
+    return np.concatenate(table(bin_order()[:, None] * (np.arange(LAGS) - LAGS // 2)[None, :] % SAMPLES), axis=0)
 
 
 def toeplitz(taps):
@@ -77,9 +82,17 @@
         acc[...] = jnp.zeros_like(acc)
 
     first = pl.multiple_of(step * depth, depth)
-    acc[...] += jnp.dot(
-        white[:, pl.ds(first, depth)].astype(jnp.bfloat16), table_ref[...], preferred_element_type=jnp.float32
-    )
+    early = white[:, pl.ds(first, depth)].astype(jnp.bfloat16).astype(jnp.float32)
+    late = white[:, pl.ds(pl.multiple_of(first + samples // 2, depth), depth)].astype(jnp.bfloat16).astype(jnp.float32)
+    for odd, folded in enumerate((early + late, early - late)):
+        part = jnp.dot(
+            folded.astype(jnp.bfloat16),
+            table_ref[:, odd * FBINS : (odd + 1) * FBINS],
+            preferred_element_type=jnp.float32,
+        )
+        half = FBINS // 2
+        acc[:, odd * half : (odd + 1) * half] += part[:, :half]
+        acc[:, FBINS + odd * half : FBINS + (odd + 1) * half] += part[:, half:]
 
     @pl.when(step == pl.num_programs(0) - 1)
     def _():
@@ -94,7 +107,7 @@
     whole = lambda *shape: pl.BlockSpec(shape, lambda i: (0,) * len(shape))
     return pl.pallas_call(
         front_kernel,
-        grid=(samples // depth,),
+        grid=(samples // 2 // depth,),
         out_shape=jax.ShapeDtypeStruct((rows * segs, 2 * FBINS), jnp.bfloat16),
         in_specs=[
             whole(segs, rows, samples),
@@ -110,12 +123,12 @@
             pltpu.VMEM((rows * segs, samples), jnp.float32),
             pltpu.VMEM((rows * segs, 2 * FBINS), jnp.float32),
         ],
-        compiler_params=pltpu.CompilerParams(vmem_limit_bytes=56 * 2**20),
+        compiler_params=pltpu.CompilerParams(vmem_limit_bytes=40 * 2**20),
         cost_estimate=pl.CostEstimate(flops=2 * 10**9, bytes_accessed=10**7, transcendentals=0),
     )(raw, band, taps, mask, jnp.asarray(dft_table()))
 
 
-PIECES = 4
+PIECES = 2
 
 
 def gather_kernel(count, own_ref, out_ref, own_sem, up_sem, down_sem, y_sem, core_sem, recv_sem):

time: 67.5 us -> 63.5 us (0.941)
  Pallas kernels: 62.2 us -> 54.9 us
  local copies, waits for them, and re-layouts: 2.48 us -> 5.66 us
    pallas_call x1, Pallas kernels: 11 us -> 4.49 us  [front(): pl.pallas_call(front_kernel, grid=(samples // 2 // depth,), out_shape=jax...]
    unnamed x6 -> x10, local copies, waits for them, and re-layouts: 0.96 us -> 4.76 us
    pallas_call x1, Pallas kernels: 31.2 us -> 30 us  [gather(): pl.pallas_call(lambda *refs: gather_kernel(count, *refs), out_shape=jax.S...]
where the time goes in v6:
time: 63.5 us; the launch traced here: 63.2 us
  Pallas kernels  54.9 us (86%)
  local copies, waits for them, and re-layouts  5.66 us (9%)
  other arithmetic  1.62 us (3%)
  between operations  0.72 us (1%)
    pallas_call x1, Pallas kernels, gather(): pl.pallas_call(lambda *refs: gather_kernel(count, *refs), out_shape=jax.S...  30 us
    pallas_call x1, Pallas kernels, back(): pl.pallas_call(back_kernel, out_shape=jax.ShapeDtypeStruct((BLOCK, rows,...  20.4 us
    unnamed x10, local copies, waits for them, and re-layouts  4.76 us
    pallas_call x1, Pallas kernels, front(): pl.pallas_call(front_kernel, grid=(samples // 2 // depth,), out_shape=jax...  4.49 us

profile of v6, /device:TPU:0, one launch (start us, length us, event | category | flops | bytes accessed | tf_op | source)
XLA Modules:
  0.0 63.2 jit_solution(2433028192999866284)
XLA Ops:
  0.7 0.7 %broadcast_compare_fusion = pred[256]{0:T(512)(128)(4,1)S(1)} fusion(s32[256]{0:T(256)} %param.12, s32[]{:T(128)} %bitcast.6), kind=kLoop, calls=%fused_computation.13 | loop fusion | flops 256 | bytes 1284 | tf_op jit(solution)/shard_map/eq | solution.py:335
  1.3 0.1 convert_reduce_fusion
  1.5 0.1 select_reduce_fusion.index_ref
  1.6 0.7 %convert_element_type.8 = f32[8,256]{1,0:T(8,128)S(1)} convert(s32[8,256]{1,0:T(8,128)} %param.11) | non-fusion elementwise | flops 2048 | bytes 16384 | tf_op jit(solution)/shard_map/convert_element_type | solution.py:331
  2.3 0.1 dynamic-slice_bitcast_fusion
  2.4 0.3 fusion
  2.6 0.1 copy.16
  2.7 0.1 reshape.14.mask_ref
  2.8 0.1 copy.18
  2.9 0.0 copy-start
  2.9 1.2 %copy-done = bf16[8,16,4096]{2,1,0:T(8,128)(2,1)S(1)} copy-done((bf16[8,16,4096]{2,1,0:T(8,128)(2,1)S(1)}, bf16[8,16,4096]{2,1,0:T(8,128)(2,1)}, u32[]{:S(2)}) %copy-start) | copy-done | bytes 1048600
  4.1 0.0 copy-start.1
  4.1 0.7 %copy-done.1 = bf16[16,64]{1,0:T(8,128)(2,1)S(1)} copy-done((bf16[16,64]{1,0:T(8,128)(2,1)S(1)}, bf16[16,64]{1,0:T(8,128)(2,1)}, u32[]{:S(2)}) %copy-start.1) | copy-done | bytes 2072
  4.8 0.0 copy-start.2
  4.8 0.7 %copy-done.2 = bf16[64]{0:T(256)(128)(2,1)S(1)} copy-done((bf16[64]{0:T(256)(128)(2,1)S(1)}, bf16[64]{0:T(256)(128)(2,1)}, u32[]{:S(2)}) %copy-start.2) | copy-done | bytes 152
  5.5 0.0 copy-start.3
  5.5 2.2 %copy-done.3 = bf16[2048,1024]{1,0:T(8,128)(2,1)S(1)} copy-done((bf16[2048,1024]{1,0:T(8,128)(2,1)S(1)}, bf16[2048,1024]{1,0:T(8,128)(2,1)}, u32[]{:S(2)}) %copy-start.3) | copy-done | bytes 4194328
  7.7 4.5 %shard_map.82.refs_0_.own_ref = bf16[128,1024]{1,0:T(8,128)(2,1)S(1)} custom-call(bf16[8,16,4096]{2,1,0:T(8,128)(2,1)S(1)} %copy-done, bf16[1,64]{1,0:T(2,128)(2,1)S(1)} %bitcast.8, bf16[16,64]{1,0:T(8,128)(2,1)S(1)} %copy-done.1, f32[128,1]{1,0:T(8,128)S(1)} %reshape.14.mask_ref, bf16[2048,1024]{1,0:T(8,128)(2,1)S(1)} %copy-done.3), custom_call_target="tpu_custom_call" | custom-call | flops 2000000000 | bytes 10000000 | tf_op jit(solution)/shard_map/pallas_call | solution.py:108
  12.2 0.0 copy-start.4
  12.2 0.6 reshape.15.scale_ref
  12.7 30.0 %shard_map.83 = bf16[16,128,1024]{2,1,0:T(8,128)(2,1)S(1)} custom-call(bf16[128,1024]{1,0:T(8,128)(2,1)S(1)} %shard_map.82.refs_0_.own_ref), custom_call_target="tpu_custom_call" | custom-call | tf_op jit(solution)/shard_map/pallas_call | solution.py:246
  42.7 0.0 copy-done.4
  42.7 20.4 %shard_map.84 = bf16[128,16,1024]{2,1,0:T(8,128)(2,1)} custom-call(s32[128]{0:T(128)S(1)} %select_reduce_fusion.index_ref, bf16[2048,1024]{1,0:T(8,128)(2,1)S(1)} %bitcast.7, bf16[128,1024]{1,0:T(8,128)(2,1)S(1)} %shard_map.82.refs_0_.own_ref, f32[2048,1]{1,0:T(8,128)S(1)} %reshape.15.scale_ref, bf16[1024,1024]{1,0:T(8,128)(2,1)S(1)} %copy-done.4), custom_call_target="tpu_custom_call" | custom-call | flops 5000000000 | bytes 10000000 | tf_op jit(solution)/shard_map/pallas_call | solution.py:303
Async XLA Ops:
  2.9 1.2 %copy-start = (bf16[8,16,4096]{2,1,0:T(8,128)(2,1)S(1)}, bf16[8,16,4096]{2,1,0:T(8,128)(2,1)}, u32[]{:S(2)}) copy-start(bf16[8,16,4096]{2,1,0:T(8,128)(2,1)} %raw_ref.1) | copy-start | bytes 3145732
  4.1 0.7 %copy-start.1 = (bf16[16,64]{1,0:T(8,128)(2,1)S(1)}, bf16[16,64]{1,0:T(8,128)(2,1)}, u32[]{:S(2)}) copy-start(bf16[16,64]{1,0:T(8,128)(2,1)} %taps_ref.1) | copy-start | bytes 6148
  4.8 0.7 %copy-start.2 = (bf16[64]{0:T(256)(128)(2,1)S(1)}, bf16[64]{0:T(256)(128)(2,1)}, u32[]{:S(2)}) copy-start(bf16[64]{0:T(256)(128)(2,1)} %param.9) | copy-start | bytes 388
  5.5 2.2 %copy-start.3 = (bf16[2048,1024]{1,0:T(8,128)(2,1)S(1)}, bf16[2048,1024]{1,0:T(8,128)(2,1)}, u32[]{:S(2)}) copy-start(bf16[2048,1024]{1,0:T(8,128)(2,1)} %constant.18.clone.table_ref) | copy-start | bytes 12582916
  12.2 30.6 %copy-start.4 = (bf16[1024,1024]{1,0:T(8,128)(2,1)S(1)}, bf16[1024,1024]{1,0:T(8,128)(2,1)}, u32[]{:S(2)}) copy-start(bf16[1024,1024]{1,0:T(8,128)(2,1)} %constant.19.clone.lag_ref) | copy-start | bytes 6291460
